TPU v7x, 768 devices: a whole 4x8x12 slice. The times are simulated.
768 devices in a mesh: dp: 4 (over x), ctx: 6 (over z_hi, core), exp: 32 (over y, z_lo).
Axes of the slice: x: 4, y: 8, z: 12 (z_hi: 3, z_lo: 4; z = z_hi * 4 + z_lo), core: 2. Of those that a mesh axis runs over, the one named last changes fastest.
Arguments:
- queries: bfloat16 [4, 768, 128, 576], P('dp', 'ctx', 'exp'), may hold values from -7 to 7
- out_grad: bfloat16 [4, 768, 128, 512], P('dp', 'ctx', 'exp'), may hold values from -6 to 6
- latent_keys: bfloat16 [4, 768, 576], P('dp', 'ctx'), may hold values from -9 to 9
- kv_gain: float32 [512], replicated, may hold values from 0.5 to 2
- query_groups: int32 [4, 6], P('dp'), may hold values from 0 to 5, each once within a row
Outputs:
- grad_queries: bfloat16 [4, 768, 128, 576], P('dp', 'ctx', 'exp')
- grad_keys: float32 [4, 6, 128, 576], P('dp', 'ctx', 'exp')
- grad_gain: float32 [512], replicated
Inputs may be any that keep to these rules, and one draw needn't show every extreme that they name: `query_groups`: each row names each group index once.
All inputs are finite; a program needn't handle non-finite values.
Results may differ from a plain program's by a relative error of at most 0.0049.
Values may be sent and summed in bfloat16 or wider, within the bound.
A program may use at most 32 MiB of HBM per device.

v0:
```python
import math

import jax
import jax.numpy as jnp
from jax import lax
from jax.sharding import PartitionSpec as P

LATENT = 512


SOFTMAX_SCALE = (0.1 * math.log(40.0) + 1.0) ** 2 / math.sqrt(192.0)
MASKED_SCORE = -1e30


def body(queries, out_grad, latent_keys, kv_gain, query_groups):
    own_keys = latent_keys[0]
    rows_q, head_count, key_width = (queries.shape[1], queries.shape[2], queries.shape[3])
    rows_k = own_keys.shape[0]
    rows_all = rows_q * head_count
    query_rows = queries[0].reshape(rows_all, key_width)
    grad_rows = out_grad[0].reshape(rows_all, LATENT)
    group_now = query_groups[0, lax.axis_index("ctx")]
    offsets = jnp.arange(rows_q, dtype=jnp.int32)
    query_pos = jnp.repeat(group_now * rows_q + offsets, head_count)
    last_row = group_now * rows_q + rows_q - 1
    ctx_count = lax.axis_size("ctx")
    key_total = rows_k * ctx_count

    def score_block(key_piece):
        scores = (
            jnp.einsum("qd,kd->qk", query_rows, key_piece, preferred_element_type=jnp.float32)
            * SOFTMAX_SCALE
        )
        grad_prob = jnp.einsum(
            "qe,ke->qk", grad_rows, key_piece[:, :LATENT], preferred_element_type=jnp.float32
        )
        key_pos = jnp.arange(key_piece.shape[0], dtype=jnp.int32)
        visible = key_pos[None, :] <= query_pos[:, None]
        return (jnp.where(visible, scores, MASKED_SCORE), grad_prob, visible)

    def keep_state(current):
        return current

    stats_init = (
        jnp.full((rows_all,), MASKED_SCORE, jnp.float32),
        jnp.zeros((rows_all,), jnp.float32),
        jnp.zeros((rows_all,), jnp.float32),
    )
    key_piece = lax.all_gather(own_keys, "ctx", axis=0, tiled=True)

    def stats_update(current):
        row_max, row_sum, weighted = current
        scores, grad_prob, visible = score_block(key_piece)
        new_max = jnp.maximum(row_max, jnp.max(scores, axis=1))
        exponent = jnp.where(visible, jnp.exp(scores - new_max[:, None]), 0.0)
        return (new_max, jnp.sum(exponent, axis=1), jnp.sum(exponent * grad_prob, axis=1))

    row_max, row_sum, weighted = lax.cond(
        jnp.int32(0) <= last_row, stats_update, keep_state, stats_init
    )
    row_delta = weighted / row_sum
    grads_init = (
        jnp.zeros((rows_all, key_width), jnp.float32),
        jnp.zeros((key_total, key_width), jnp.float32),
    )
    grads_key_piece = lax.all_gather(own_keys, "ctx", axis=0, tiled=True)

    def grads_update(current):
        scores, grad_prob, visible = score_block(grads_key_piece)
        weights = jnp.where(visible, jnp.exp(scores - row_max[:, None]) / row_sum[:, None], 0.0)
        dscore = (weights * (grad_prob - row_delta[:, None])).astype(jnp.bfloat16)
        weights_low = weights.astype(jnp.bfloat16)
        grad_query = (
            jnp.dot(dscore, grads_key_piece, preferred_element_type=jnp.float32) * SOFTMAX_SCALE
        )
        key_part = (
            jnp.einsum("qk,qd->kd", dscore, query_rows, preferred_element_type=jnp.float32)
            * SOFTMAX_SCALE
        )
        value_part = jnp.einsum(
            "qk,qe->ke", weights_low, grad_rows, preferred_element_type=jnp.float32
        )
        key_part = key_part + jnp.pad(value_part, ((0, 0), (0, key_width - LATENT)))
        return (grad_query, key_part)

    grad_query, grad_keys = lax.cond(jnp.int32(0) <= last_row, grads_update, keep_state, grads_init)
    grad_queries = grad_query.astype(jnp.bfloat16).reshape(1, rows_q, head_count, key_width)
    exp_count = lax.axis_size("exp")
    share = rows_k // exp_count
    summed = lax.psum_scatter(grad_keys, ("ctx", "exp"), scatter_dimension=0, tiled=True).reshape(
        1, share, key_width
    )
    key_slice = lax.dynamic_slice_in_dim(own_keys, lax.axis_index("exp") * share, share, 0)
    gain_terms = jnp.sum(summed[0, :, :LATENT] * key_slice[:, :LATENT].astype(jnp.float32), axis=0)
    grad_gain = lax.psum(gain_terms, ("dp", "ctx", "exp")) / kv_gain
    return (grad_queries, summed.reshape(1, 1, share, key_width), grad_gain)


def solution(mesh):
    in_specs = (
        P("dp", "ctx", "exp", None),
        P("dp", "ctx", "exp", None),
        P("dp", "ctx", None),
        P(),
        P("dp", None),
    )
    out_specs = (P("dp", "ctx", "exp", None), P("dp", "ctx", "exp", None), P())
    return jax.shard_map(body, mesh=mesh, in_specs=in_specs, out_specs=out_specs, check_vma=False)
```

profile of v0, /device:TPU:1, one launch (start us, length us, event | category | flops | bytes accessed | tf_op | source)
XLA Modules:
  0.0 481.2 jit_solution(12286212605718180520)
XLA Ops:
  7.2 1.3 fusion.9
  8.5 0.6 iota_add_fusion
  9.2 1.6 copy.20
  10.8 0.3 reshape_squeeze.6
  11.3 30.2 %all-gather = bf16[1,768,576]{2,1,0:T(8,128)(2,1)S(1)} all-gather(bf16[1,128,576]{2,1,0:T(8,128)(2,1)S(1)} %copy.21), channel_id=2, replica_groups=mesh['dp'=4,'ctx'=6,'exp'=32] {'ctx'}, dimensions={1}, use_global_device_ids=true | all-gather | bytes 1032192 | tf_op jit(solution)/shard_map/all_gather | solution.py:66
  42.3 4.4 conditional.2
  42.5 1.0 fusion.8
  43.4 0.6 broadcast_maximum_fusion
  44.0 1.5 multiply_reduce_fusion
  45.5 1.2 fusion
  46.8 6.8 %conditional.3 = (f32[768,576]{0,1:T(8,128)S(1)}, bf16[1,128,4,576]{1,3,2,0:T(8,128)(2,1)}) conditional(s32[]{:T(128)} %convert_element_type.24, () %tuple.28, (s32[128,4]{1,0:T(8,128)S(1)}, bf16[512,576]{1,0:T(8,128)(2,1)S(1)}, bf16[768,576]{1,0:T(8,128)(2,1)S(1)}, f32[512]{0:T(512)}, f32[512]{0:T(512)S(1)}, ...), branch_computations={%region_5.6_spmd, %region_6.7_spmd} | conditional | flops 2169668096 | bytes 25643080 | solution.py:86
  46.9 1.8 divide_select_fusion
  48.7 0.6 multiply_convert_fusion
  49.3 0.6 fusion.3
  50.0 0.4 copy-done.1
  50.4 0.7 pad_add_fusion
  51.1 0.7 fusion.2
  52.3 1.3 copy.26
  53.6 1.8 copy.22
  55.6 1.3 dynamic-slice.1
  57.5 305.4 %all-reduce.4.cloned.1.call-done = f32[768,576]{1,0:T(8,128)} async-done(((f32[768,576]{1,0:T(8,128)}), f32[768,576]{1,0:T(8,128)}) %all-reduce.4.cloned.1.call-update) | async-done | bytes 1769488
  362.9 1.3 dynamic-slice_bitcast_fusion
  364.3 109.5 %psum.7 = f32[512]{0:T(512)S(1)} all-reduce(f32[512]{0:T(512)S(1)} %fusion.7), channel_id=1, replica_groups=mesh['dp'=4,'ctx'=6,'exp'=32] {'dp','ctx','exp'}, use_global_device_ids=true, to_apply=%region_9.10 | all-reduce | flops 512 | bytes 4096 | tf_op jit(solution)/shard_map/psum | solution.py:95
  473.8 0.6 div.18
  (22 shorter events, 1.4 us)
Async XLA Ops:
  7.2 3.9 copy-start.2
  7.2 355.7 %all-reduce.4.cloned.1.call-start = ((), (), s32[]{:S(2)}) async-start(), calls=%async_computation | async-start | bytes 3932160
  10.7 30.7 %copy-start.3 = (bf16[1,128,4,512]{3,2,1,0:T(4,128)(2,1)S(1)}, bf16[1,128,4,512]{3,2,1,0:T(4,128)(2,1)}, u32[]{:S(2)}) copy-start(bf16[1,128,4,512]{3,2,1,0:T(4,128)(2,1)} %param.10) | copy-start | bytes 1572868
  46.8 1.9 copy-start
  49.3 1.1 copy-start.1
  55.3 418.5 %copy-start.4 = (f32[512]{0:T(512)S(1)}, f32[512]{0:T(512)}, u32[]{:S(2)}) copy-start(f32[512]{0:T(512)} %param.12) | copy-start | bytes 6148
Sparse Core Ops, SparseCore 0:
  55.5 307.3 all-reduce.3
where the time goes:
time: 482 us; the launch traced here: 481 us
  waiting for transfers between devices  305 us (63%)
  blocking collectives  140 us (29%)
  between operations  15.4 us (3%)
  local copies, waits for them, and re-layouts  9.31 us (2%)
  matrix products  6.86 us (1%)
    unnamed x2, waiting for transfers between devices  305 us
    psum x1, blocking collectives, body(): grad_gain = lax.psum(gain_terms, ('dp', 'ctx', 'exp')) / kv_gain  110 us
    all_gather x1, blocking collectives, body(): grads_key_piece = lax.all_gather(own_keys, 'ctx', axis=0, tiled=True)  30.2 us
  transfers between devices with their start and end apart: 1, of which 1 were waited for; matrix products, arithmetic and copies ran while one was open for 0% of the time, Pallas kernels for 0%

commit v1 on v0

v1 whole, which is shorter than its diff:
```python
import math

import jax
import jax.numpy as jnp
from jax import lax
from jax.experimental import pallas as pl
from jax.experimental.pallas import tpu as pltpu
from jax.sharding import PartitionSpec as P

LATENT = 512
WIDTH = 576
ROPE = WIDTH - LATENT
SCALE = (0.1 * math.log(40.0) + 1.0) ** 2 / math.sqrt(192.0)
MASKED = -1e30
MESH_ID = pl.DeviceIdType.MESH
F32 = jnp.float32
BF16 = jnp.bfloat16

X, Y, ZH, ZL, CORES = 4, 8, 3, 4, 2
QUARTER = WIDTH // 4
PIECES = ((0, 80), (80, 64))
Y_PEERS = (4, 3, 5, 2, 6, 1, 7)
Z_PEERS = tuple((rel, d) for rel in (1, 2, 0) for d in range(ZL) if (rel, d) != (0, 0))
X_PEERS = ((0, 1), (1, 0), (3, 0), (2, 0), (1, 1), (3, 1), (2, 1))
COLS_Y = 384
NT = (((1,), (1,)), ((), ()))
NN = (((1,), (0,)), ((), ()))


def dot(a, b, dims=NN):
    return lax.dot_general(a, b, dims, preferred_element_type=F32)


def kernel(
    q_hbm, do_hbm, kt_hbm, gain_ref, groups_ref,
    gq_hbm, gk_ref, gg_ref,
    qp, do_raw, do_f32, dop, kt, kr, st, dpt, ds, pw,
    stat, stat_in, h1, h2, h1_in, h2_in, t1, h1b, h1b_in, t2, t2_in,
    ga, ga_in, gb, gb_in, gc, gc_in, dq, dq_in, gq,
    local_sem, send_sem, recv_sem,
):
    x = lax.axis_index("dp")
    ctx = lax.axis_index("ctx")
    exp = lax.axis_index("exp")
    zh, core = ctx // CORES, ctx % CORES
    y, zl = exp // ZL, exp % ZL

    def device(dx=0, dy=0, dh=0, dl=0, dc=0):
        return (
            (x + dx) % X,
            ((zh + dh) % ZH) * CORES + (core + dc) % CORES,
            ((y + dy) % Y) * ZL + (zl + dl) % ZL,
        )

    count = [0]

    def remote(src, dst, **where):
        i = count[0]
        count[0] += 1
        return pltpu.make_async_remote_copy(
            src_ref=src, dst_ref=dst, send_sem=send_sem.at[i], recv_sem=recv_sem.at[i],
            device_id=device(**where), device_id_type=MESH_ID,
        )

    loads = [pltpu.make_async_copy(kt_hbm, kt.at[0], local_sem.at[0])]
    loads.append(pltpu.make_async_copy(do_hbm, do_raw, local_sem.at[1]))
    for h in range(4):
        loads.append(
            pltpu.make_async_copy(
                q_hbm.at[h], qp.at[h // 2, :, pl.ds((h % 2) * 128, 128)], local_sem.at[2 + h]
            )
        )
    for copy in loads:
        copy.start()

    barrier = pltpu.get_barrier_semaphore()
    peers = [dict(dh=rel, dl=d) for rel, d in Z_PEERS]
    peers += [dict(dy=d) for d in Y_PEERS]
    peers += [dict(dx=d, dc=c) for d, c in X_PEERS]
    for peer in peers:
        pl.semaphore_signal(barrier, inc=1, device_id=device(**peer), device_id_type=MESH_ID)
    loads[0].wait()
    pl.semaphore_wait(barrier, len(peers))

    p0 = (y % 4) * QUARTER
    first = {}
    for at, (off, rows) in enumerate(PIECES):
        for rel in (1, 2):
            part = pl.ds(pl.multiple_of(p0 + off, 16), rows)
            first[rel, at] = remote(kt.at[0, part], kt.at[rel, part], dh=ZH - rel)
            first[rel, at].start()

    for copy in loads[2:]:
        copy.wait()
    swap_q = remote(qp.at[pl.ds(0, 2)], qp.at[pl.ds(2, 2)], dc=1)
    swap_q.start()
    loads[1].wait()
    do_f32[...] = do_raw[...].astype(F32)
    for h in range(4):
        dop[h // 2, pl.ds((h % 2) * 128, 128), :] = do_f32[:, h, :].astype(BF16)
    swap_do = remote(dop.at[pl.ds(0, 2)], dop.at[pl.ds(2, 2)], dc=1)
    swap_do.start()

    second = []
    for at, (off, rows) in enumerate(PIECES):
        for rel in (1, 2):
            first[rel, at].wait_recv()
            part = pl.ds(pl.multiple_of(p0 + off, 16), rows)
            for dy in (1, Y - 1, 2 if at == 0 else Y - 2):
                copy = remote(kt.at[rel, part], kt.at[rel, part], dy=dy)
                copy.start()
                second.append(copy)

    swap_q.wait_recv()
    swap_do.wait_recv()

    def keys_in(rel):
        for c in range(0, LATENT, 128):
            kr[rel, :, c : c + 128] = kt[rel, c : c + 128, :].astype(F32).T.astype(BF16)
        kr[rel, :, LATENT:] = kt[rel, LATENT:, :].astype(F32).T.astype(BF16)

    diff = lax.broadcasted_iota(jnp.int32, (128, 256), 0) - (
        lax.broadcasted_iota(jnp.int32, (128, 256), 1) & 127
    )
    group = (groups_ref[0, ctx], groups_ref[0, zh * CORES + 1 - core])

    def score(rel):
        base = ((zh + rel) % ZH) * CORES + core
        keys = kr[rel]
        for cc in range(4):
            visible = diff <= (group[cc // 2] - base) * 128
            s = dot(keys, qp[cc]) * SCALE
            st[cc, pl.ds(rel * 128, 128), :] = jnp.where(visible, s, MASKED)
            dpt[cc, pl.ds(rel * 128, 128), :] = dot(keys[:, :LATENT], dop[cc], NT)

    keys_in(0)
    score(0)
    for copy in second:
        copy.wait_recv()
    for rel in (1, 2):
        keys_in(rel)
        score(rel)

    for cc in range(4):
        s = st[cc]
        m = jnp.max(s, axis=0, keepdims=True)
        p = jnp.where(s > 0.5 * MASKED, jnp.exp(s - m), 0.0)
        st[cc] = p
        stat[cc, 0:1, :] = m
        stat[cc, 1:2, :] = jnp.sum(p, axis=0, keepdims=True)
        stat[cc, 2:3, :] = jnp.sum(p * dpt[cc], axis=0, keepdims=True)
        stat[cc, 3:8, :] = jnp.zeros((5, 256), F32)
    swap_stat = remote(stat, stat_in, dc=1)
    swap_stat.start()
    swap_stat.wait_recv()

    for cc in range(4):
        other = (cc + 2) % 4
        m0, l0, w0 = stat[cc, 0:1, :], stat[cc, 1:2, :], stat[cc, 2:3, :]
        m1, l1, w1 = stat_in[other, 0:1, :], stat_in[other, 1:2, :], stat_in[other, 2:3, :]
        m = jnp.maximum(m0, m1)
        e0, e1 = jnp.exp(m0 - m), jnp.exp(m1 - m)
        inv = 1.0 / (l0 * e0 + l1 * e1)
        delta = (w0 * e0 + w1 * e1) * inv
        w = st[cc] * (e0 * inv)
        pw[cc] = w.astype(BF16)
        ds[cc] = (w * (dpt[cc] - delta)).astype(BF16)

    out_row = lax.broadcasted_iota(jnp.int32, (128, 128), 0)
    in_row = lax.broadcasted_iota(jnp.int32, (128, 128), 1)
    wanted = ((out_row & 31) >> 2) * 16 + (out_row >> 5) * 4 + (out_row & 3)
    by_z = (in_row == wanted).astype(BF16)
    gain = jnp.zeros((1, LATENT), F32)
    for rel in range(3):
        rows = pl.ds(rel * 128, 128)
        dk = dot(ds[0, rows, :], qp[0], NT)
        dv = dot(pw[0, rows, :], dop[0])
        for cc in range(1, 4):
            dk = dk + dot(ds[cc, rows, :], qp[cc], NT)
            dv = dv + dot(pw[cc, rows, :], dop[cc])
        dk = dk * SCALE
        full = dk[:, :LATENT] + dv
        gain = gain + jnp.sum(full * kr[rel, :, :LATENT].astype(F32), axis=0, keepdims=True)
        h1[rel] = full[:, :COLS_Y].astype(BF16)
        h2[rel, :, 0:128] = dot(by_z, full[:, COLS_Y:].astype(BF16)).astype(BF16)
        h2[rel, :, 128 : 128 + ROPE] = dot(by_z, dk[:, LATENT:].astype(BF16)).astype(BF16)
        h2[rel, :, 128 + ROPE :] = jnp.zeros((128, 128 - ROPE), BF16)

    def pack(row, ref):
        for t in range(4):
            ref[t : t + 1, :] = row[:, t * 128 : (t + 1) * 128]
        ref[4:8, :] = jnp.zeros((4, 128), F32)

    pack(gain, ga)
    gain_a = [remote(ga, ga_in.at[i], dx=d, dc=c) for i, (d, c) in enumerate(X_PEERS)]
    for copy in gain_a:
        copy.start()

    def y_rows(dy):
        return pl.ds(pl.multiple_of(((y + dy) % Y) * 16, 16), 16)

    def z_rows(dl):
        return pl.ds(pl.multiple_of(((zl + dl) % ZL) * 32, 32), 32)

    stage_y = [remote(h1.at[:, y_rows(d), :], h1_in.at[i], dy=d) for i, d in enumerate(Y_PEERS)]
    stage_z = [
        remote(h2.at[rel, z_rows(d), :], h2_in.at[i], dh=rel, dl=d)
        for i, (rel, d) in enumerate(Z_PEERS)
    ]
    for i in range(len(Z_PEERS)):
        stage_z[i].start()
        if i < len(Y_PEERS):
            stage_y[i].start()

    def query_part(cc):
        total = dot(kt[0], ds[cc, 0:128, :])
        for rel in (1, 2):
            total = total + dot(kt[rel], ds[cc, rel * 128 : rel * 128 + 128, :])
        return total * SCALE

    swap_dq = []
    for cc in (2, 3):
        dq[cc - 2] = query_part(cc)
        copy = remote(dq.at[cc - 2], dq_in.at[cc - 2], dc=1)
        copy.start()
        swap_dq.append(copy)

    for copy in gain_a:
        copy.wait_recv()
    total = ga[...]
    for i in range(len(X_PEERS)):
        total = total + ga_in[i]
    gb[...] = total
    gain_b = [remote(gb, gb_in.at[i], dy=d) for i, d in enumerate(Y_PEERS)]
    for copy in gain_b:
        copy.start()

    stores = []
    for cc in range(2):
        own = query_part(cc)
        swap_dq[cc].wait_recv()
        gq[cc] = (own + dq_in[cc]).astype(BF16)
        for h in range(2):
            store = pltpu.make_async_copy(
                gq.at[cc, :, pl.ds(h * 128, 128)], gq_hbm.at[cc * 2 + h],
                local_sem.at[6 + cc * 2 + h],
            )
            store.start()
            stores.append(store)

    t1[...] = jnp.zeros_like(t1)
    for copy in stage_y:
        copy.wait_recv()
    for rel in range(3):
        part = h1[rel, y_rows(0), :].astype(F32)
        for i in range(len(Y_PEERS)):
            part = part + h1_in[i, rel].astype(F32)
        for l in range(ZL):
            for t in range(3):
                t1[rel, l, t * 4 : t * 4 + 4, :] = part[l * 4 : l * 4 + 4, t * 128 : (t + 1) * 128]
    h1b[...] = t1[...].astype(BF16)
    stage_yz = [
        remote(h1b.at[rel, (zl + d) % ZL], h1b_in.at[i], dh=rel, dl=d)
        for i, (rel, d) in enumerate(Z_PEERS)
    ]
    for copy in stage_yz:
        copy.start()

    for copy in stage_z:
        copy.wait_recv()
    part = h2[0, z_rows(0), :].astype(F32)
    for i in range(len(Z_PEERS)):
        part = part + h2_in[i].astype(F32)
    for yy in range(Y):
        for t in range(2):
            t2[yy, t * 4 : t * 4 + 4, :] = part[yy * 4 : yy * 4 + 4, t * 128 : (t + 1) * 128]
    stage_zy = [remote(t2.at[(y + d) % Y], t2_in.at[i], dy=d) for i, d in enumerate(Y_PEERS)]
    for copy in stage_zy:
        copy.start()

    for copy in gain_b:
        copy.wait_recv()
    total = gb[...]
    for i in range(len(Y_PEERS)):
        total = total + gb_in[i]
    gc[...] = total
    gain_c = [remote(gc, gc_in.at[i], dh=rel, dl=d) for i, (rel, d) in enumerate(Z_PEERS)]
    for copy in gain_c:
        copy.start()

    for copy in stage_yz:
        copy.wait_recv()
    part = t1[0, zl]
    for i in range(len(Z_PEERS)):
        part = part + h1b_in[i].astype(F32)
    for t in range(3):
        gk_ref[:, t * 128 : (t + 1) * 128] = part[t * 4 : t * 4 + 4, :]
    for copy in stage_zy:
        copy.wait_recv()
    part = t2[y]
    for i in range(len(Y_PEERS)):
        part = part + t2_in[i]
    gk_ref[:, COLS_Y:LATENT] = part[0:4, :]
    gk_ref[:, LATENT:] = part[4:8, :ROPE]
    for copy in gain_c:
        copy.wait_recv()
    total = gc[...]
    for i in range(len(Z_PEERS)):
        total = total + gc_in[i]
    gg_ref[...] = total[0:4, :] / gain_ref[...]

    for copy in stores:
        copy.wait()
    sent = list(first.values()) + second + [swap_q, swap_do, swap_stat] + swap_dq
    sent += gain_a + gain_b + gain_c + stage_y + stage_z + stage_yz + stage_zy
    for copy in sent:
        copy.wait_send()


N_COPIES = 4 + 12 + 3 + 2 + len(X_PEERS) + 3 * len(Y_PEERS) + 3 * len(Z_PEERS)


def body(queries, out_grad, latent_keys, kv_gain, query_groups):
    q_t = jnp.transpose(queries[0], (1, 2, 0))
    k_t = jnp.transpose(latent_keys[0], (1, 0))
    any_spec = pl.BlockSpec(memory_space=pl.ANY)
    vmem_spec = pl.BlockSpec(memory_space=pltpu.VMEM)
    ny, nz, nx = len(Y_PEERS), len(Z_PEERS), len(X_PEERS)
    gq, gk, gg = pl.pallas_call(
        kernel,
        out_shape=(
            jax.ShapeDtypeStruct((4, WIDTH, 128), BF16),
            jax.ShapeDtypeStruct((4, WIDTH), F32),
            jax.ShapeDtypeStruct((4, 128), F32),
        ),
        in_specs=[any_spec, any_spec, any_spec, vmem_spec, pl.BlockSpec(memory_space=pltpu.SMEM)],
        out_specs=(any_spec, vmem_spec, vmem_spec),
        scratch_shapes=[
            pltpu.VMEM((4, WIDTH, 256), BF16),
            pltpu.VMEM((128, 4, LATENT), BF16),
            pltpu.VMEM((128, 4, LATENT), F32),
            pltpu.VMEM((4, 256, LATENT), BF16),
            pltpu.VMEM((3, WIDTH, 128), BF16),
            pltpu.VMEM((3, 128, WIDTH), BF16),
            pltpu.VMEM((4, 384, 256), F32),
            pltpu.VMEM((4, 384, 256), F32),
            pltpu.VMEM((4, 384, 256), BF16),
            pltpu.VMEM((4, 384, 256), BF16),
            pltpu.VMEM((4, 8, 256), F32),
            pltpu.VMEM((4, 8, 256), F32),
            pltpu.VMEM((3, 128, COLS_Y), BF16),
            pltpu.VMEM((3, 128, 256), BF16),
            pltpu.VMEM((ny, 3, 16, COLS_Y), BF16),
            pltpu.VMEM((nz, 32, 256), BF16),
            pltpu.VMEM((3, ZL, 16, 128), F32),
            pltpu.VMEM((3, ZL, 16, 128), BF16),
            pltpu.VMEM((nz, 16, 128), BF16),
            pltpu.VMEM((Y, 8, 128), F32),
            pltpu.VMEM((ny, 8, 128), F32),
            pltpu.VMEM((8, 128), F32),
            pltpu.VMEM((nx, 8, 128), F32),
            pltpu.VMEM((8, 128), F32),
            pltpu.VMEM((ny, 8, 128), F32),
            pltpu.VMEM((8, 128), F32),
            pltpu.VMEM((nz, 8, 128), F32),
            pltpu.VMEM((2, WIDTH, 256), F32),
            pltpu.VMEM((2, WIDTH, 256), F32),
            pltpu.VMEM((2, WIDTH, 256), BF16),
            pltpu.SemaphoreType.DMA((10,)),
            pltpu.SemaphoreType.DMA((N_COPIES,)),
            pltpu.SemaphoreType.DMA((N_COPIES,)),
        ],
        compiler_params=pltpu.CompilerParams(
            collective_id=0, has_side_effects=True, vmem_limit_bytes=48 * 2**20
        ),
        cost_estimate=pl.CostEstimate(
            flops=5 * 2 * 512 * 768 * 550, bytes_accessed=3 * 2**20, transcendentals=512 * 768
        ),
        name="mla_backward",
    )(q_t, out_grad[0], k_t, kv_gain.reshape(4, 128), query_groups)
    grad_queries = jnp.transpose(gq, (2, 0, 1))[None]
    return grad_queries, gk.reshape(1, 1, 4, WIDTH), gg.reshape(LATENT)


def solution(mesh):
    in_specs = (
        P("dp", "ctx", "exp", None),
        P("dp", "ctx", "exp", None),
        P("dp", "ctx", None),
        P(),
        P("dp", None),
    )
    out_specs = (P("dp", "ctx", "exp", None), P("dp", "ctx", "exp", None), P())
    return jax.shard_map(body, mesh=mesh, in_specs=in_specs, out_specs=out_specs, check_vma=False)
```

time: 482 us -> 59.7 us (0.12)
  waiting for transfers between devices: 305 us -> 0 us
  blocking collectives: 140 us -> 0 us
  Pallas kernels: 0 us -> 53.1 us
  between operations: 15.4 us -> 0.66 us
  matrix products: 6.86 us -> 0 us
    unnamed x2 -> x0, waiting for transfers between devices: 305 us -> none
    psum x1 -> x0, blocking collectives: 110 us -> none  [body(): grad_gain = lax.psum(gain_terms, ('dp', 'ctx', 'exp')) / kv_gain]
    pallas_call x0 -> x1, Pallas kernels: none -> 53.1 us  [body(): pl.pallas_call(kernel, out_shape=(jax.ShapeDtypeStruct((4, WIDTH, 128), B...]
    all_gather x1 -> x0, blocking collectives: 30.2 us -> none  [body(): grads_key_piece = lax.all_gather(own_keys, 'ctx', axis=0, tiled=True)]
    dot_general x7 -> x0, matrix products: 6.86 us -> none  [the longest x2 2.71 us: score_block(): jnp.einsum('qd,kd->qk', query_rows, key_piece, preferred_element_type=jnp...]
  transfers between devices with their start and end apart: 1 -> 0, of which waited for: 1 -> 0; matrix products, arithmetic and copies ran while one was open for 0% -> 0% of each run, Pallas kernels for 0% -> 0%
where the time goes in v1:
time: 59.7 us; the launch traced here: 59.4 us
  Pallas kernels  53.1 us (89%)
  local copies, waits for them, and re-layouts  5.68 us (10%)
  between operations  0.66 us (1%)
    pallas_call x1, Pallas kernels, body(): pl.pallas_call(kernel, out_shape=(jax.ShapeDtypeStruct((4, WIDTH, 128), B...  53.1 us
    unnamed x13, local copies, waits for them, and re-layouts  5.68 us

profile of v1, /device:TPU:1, one launch (start us, length us, event | category | flops | bytes accessed | tf_op | source)
XLA Modules:
  0.0 59.4 jit_solution(1061823968451986804)
XLA Ops:
  0.6 0.0 copy-start.3
  0.6 0.0 copy-start.4
  0.7 0.7 %copy-done.3 = f32[512]{0:T(512)S(1)} copy-done((f32[512]{0:T(512)S(1)}, f32[512]{0:T(512)}, u32[]{:S(2)}) %copy-start.3) | copy-done | bytes 2072
  1.3 0.0 copy-done.4
  1.3 0.0 copy-start
  1.3 1.1 %copy-done = bf16[1,128,4,576]{1,3,2,0:T(8,128)(2,1)S(1)} copy-done((bf16[1,128,4,576]{1,3,2,0:T(8,128)(2,1)S(1)}, bf16[1,128,4,576]{1,3,2,0:T(8,128)(2,1)}, u32[]{:S(2)}) %copy-start) | copy-done | bytes 589848
  2.4 0.0 copy-start.1
  2.4 1.0 %copy-done.1 = bf16[1,128,4,512]{3,2,1,0:T(4,128)(2,1)S(1)} copy-done((bf16[1,128,4,512]{3,2,1,0:T(4,128)(2,1)S(1)}, bf16[1,128,4,512]{3,2,1,0:T(4,128)(2,1)}, u32[]{:S(2)}) %copy-start.1) | copy-done | bytes 524312
  3.4 0.0 copy-start.2
  3.4 0.9 %copy-done.2 = bf16[1,128,576]{1,2,0:T(8,128)(2,1)S(1)} copy-done((bf16[1,128,576]{1,2,0:T(8,128)(2,1)S(1)}, bf16[1,128,576]{1,2,0:T(8,128)(2,1)}, u32[]{:S(2)}) %copy-start.2) | copy-done | bytes 147480
  4.3 53.1 %mla_backward.1 = (bf16[4,576,128]{2,1,0:T(8,128)(2,1)S(1)}, f32[4,576]{1,0:T(4,128)S(1)}, f32[4,128]{1,0:T(4,128)S(1)}) custom-call(bf16[4,576,128]{2,1,0:T(8,128)(2,1)S(1)} %bitcast.16, bf16[128,4,512]{2,1,0:T(4,128)(2,1)S(1)} %bitcast.17, bf16[576,128]{1,0:T(8,128)(2,1)S(1)} %bitcast.18, f32[4,128]{1,0:T(4,128)S(1)} %bitcast.19, s32[1,6]{1,0:T(1,128)S(1)} %copy-done.4), custom_call_target="tpu_custom_call" | custom-call | flops 2162688000 | bytes 3145728 | tf_op jit(solution)/shard_map/mla_backward/pallas_call | solution.py:329
  57.4 0.8 %copy.11 = bf16[1,128,4,576]{1,3,2,0:T(8,128)(2,1)} copy(bf16[1,128,4,576]{1,3,2,0:T(8,128)(2,1)S(1)} %bitcast.13) | data formatting | bytes 1179648
  58.3 0.6 %copy.12 = f32[1,1,4,576]{3,2,1,0:T(4,128)} copy(f32[1,1,4,576]{3,2,1,0:T(4,128)S(1)} %bitcast.14) | data formatting | bytes 18432
  58.9 0.6 copy.13
Async XLA Ops:
  0.6 0.7 %copy-start.3 = (f32[512]{0:T(512)S(1)}, f32[512]{0:T(512)}, u32[]{:S(2)}) copy-start(f32[512]{0:T(512)} %param.8) | copy-start | bytes 6148
  0.6 0.7 %copy-start.4 = (s32[1,6]{1,0:T(1,128)S(1)}, s32[1,6]{1,0:T(1,128)}, u32[]{:S(2)}) copy-start(s32[1,6]{1,0:T(1,128)} %groups_ref.1) | copy-start | bytes 76
  1.3 1.1 %copy-start = (bf16[1,128,4,576]{1,3,2,0:T(8,128)(2,1)S(1)}, bf16[1,128,4,576]{1,3,2,0:T(8,128)(2,1)}, u32[]{:S(2)}) copy-start(bf16[1,128,4,576]{1,3,2,0:T(8,128)(2,1)} %param.5) | copy-start | bytes 1769476
  2.4 1.0 %copy-start.1 = (bf16[1,128,4,512]{3,2,1,0:T(4,128)(2,1)S(1)}, bf16[1,128,4,512]{3,2,1,0:T(4,128)(2,1)}, u32[]{:S(2)}) copy-start(bf16[1,128,4,512]{3,2,1,0:T(4,128)(2,1)} %param.6) | copy-start | bytes 1572868
  3.4 0.9 %copy-start.2 = (bf16[1,128,576]{1,2,0:T(8,128)(2,1)S(1)}, bf16[1,128,576]{1,2,0:T(8,128)(2,1)}, u32[]{:S(2)}) copy-start(bf16[1,128,576]{1,2,0:T(8,128)(2,1)} %param.7) | copy-start | bytes 442372

commit v2 on v1

--- a/solution.py
+++ b/solution.py
@@ -20,7 +20,8 @@
 QUARTER = WIDTH // 4
 PIECES = ((0, 80), (80, 64))
 Y_PEERS = (4, 3, 5, 2, 6, 1, 7)
-Z_PEERS = tuple((rel, d) for rel in (1, 2, 0) for d in range(ZL) if (rel, d) != (0, 0))
+Z_PEERS = (6, 5, 7, 4, 8, 3, 9, 2, 10, 1, 11)
+Z_FAR = 5
 X_PEERS = ((0, 1), (1, 0), (3, 0), (2, 0), (1, 1), (3, 1), (2, 1))
 COLS_Y = 384
 NT = (((1,), (1,)), ((), ()))
@@ -45,11 +46,12 @@
     zh, core = ctx // CORES, ctx % CORES
     y, zl = exp // ZL, exp % ZL
 
-    def device(dx=0, dy=0, dh=0, dl=0, dc=0):
+    def device(dx=0, dy=0, dz=0, dc=0):
+        z = (zh * ZL + zl + dz) % (ZH * ZL)
         return (
             (x + dx) % X,
-            ((zh + dh) % ZH) * CORES + (core + dc) % CORES,
-            ((y + dy) % Y) * ZL + (zl + dl) % ZL,
+            (z // ZL) * CORES + (core + dc) % CORES,
+            ((y + dy) % Y) * ZL + z % ZL,
         )
 
     count = [0]
@@ -74,7 +76,7 @@
         copy.start()
 
     barrier = pltpu.get_barrier_semaphore()
-    peers = [dict(dh=rel, dl=d) for rel, d in Z_PEERS]
+    peers = [dict(dz=d) for d in Z_PEERS]
     peers += [dict(dy=d) for d in Y_PEERS]
     peers += [dict(dx=d, dc=c) for d, c in X_PEERS]
     for peer in peers:
@@ -84,10 +86,10 @@
 
     p0 = (y % 4) * QUARTER
     first = {}
-    for at, (off, rows) in enumerate(PIECES):
-        for rel in (1, 2):
+    for rel in (1, 2):
+        for at, (off, rows) in enumerate(PIECES):
             part = pl.ds(pl.multiple_of(p0 + off, 16), rows)
-            first[rel, at] = remote(kt.at[0, part], kt.at[rel, part], dh=ZH - rel)
+            first[rel, at] = remote(kt.at[0, part], kt.at[rel, part], dz=(ZH - rel) * ZL)
             first[rel, at].start()
 
     for copy in loads[2:]:
@@ -101,15 +103,15 @@
     swap_do = remote(dop.at[pl.ds(0, 2)], dop.at[pl.ds(2, 2)], dc=1)
     swap_do.start()
 
-    second = []
-    for at, (off, rows) in enumerate(PIECES):
-        for rel in (1, 2):
+    second = {1: [], 2: []}
+    for rel in (1, 2):
+        for at, (off, rows) in enumerate(PIECES):
             first[rel, at].wait_recv()
             part = pl.ds(pl.multiple_of(p0 + off, 16), rows)
             for dy in (1, Y - 1, 2 if at == 0 else Y - 2):
                 copy = remote(kt.at[rel, part], kt.at[rel, part], dy=dy)
                 copy.start()
-                second.append(copy)
+                second[rel].append(copy)
 
     swap_q.wait_recv()
     swap_do.wait_recv()
@@ -135,9 +137,9 @@
 
     keys_in(0)
     score(0)
-    for copy in second:
-        copy.wait_recv()
     for rel in (1, 2):
+        for copy in second[rel]:
+            copy.wait_recv()
         keys_in(rel)
         score(rel)
 
@@ -166,12 +168,17 @@
         pw[cc] = w.astype(BF16)
         ds[cc] = (w * (dpt[cc] - delta)).astype(BF16)
 
-    out_row = lax.broadcasted_iota(jnp.int32, (128, 128), 0)
-    in_row = lax.broadcasted_iota(jnp.int32, (128, 128), 1)
-    wanted = ((out_row & 31) >> 2) * 16 + (out_row >> 5) * 4 + (out_row & 3)
-    by_z = (in_row == wanted).astype(BF16)
+    def picks(rows, wanted):
+        out_row = lax.broadcasted_iota(jnp.int32, (rows, 128), 0)
+        in_row = lax.broadcasted_iota(jnp.int32, (rows, 128), 1)
+        return (in_row == wanted(out_row)).astype(BF16)
+
+    by_z = picks(128, lambda o: ((o & 31) >> 2) * 16 + (o >> 5) * 4 + (o & 3))
+    by_z_low = picks(64, lambda o: ((o & 15) >> 2) * 16 + (o >> 4) * 4 + (o & 3))
+    by_z_high = picks(64, lambda o: (((o & 15) >> 2) + 4) * 16 + (o >> 4) * 4 + (o & 3))
     gain = jnp.zeros((1, LATENT), F32)
-    for rel in range(3):
+
+    def key_part(rel, gain):
         rows = pl.ds(rel * 128, 128)
         dk = dot(ds[0, rows, :], qp[0], NT)
         dv = dot(pw[0, rows, :], dop[0])
@@ -180,37 +187,44 @@
             dv = dv + dot(pw[cc, rows, :], dop[cc])
         dk = dk * SCALE
         full = dk[:, :LATENT] + dv
-        gain = gain + jnp.sum(full * kr[rel, :, :LATENT].astype(F32), axis=0, keepdims=True)
         h1[rel] = full[:, :COLS_Y].astype(BF16)
-        h2[rel, :, 0:128] = dot(by_z, full[:, COLS_Y:].astype(BF16)).astype(BF16)
-        h2[rel, :, 128 : 128 + ROPE] = dot(by_z, dk[:, LATENT:].astype(BF16)).astype(BF16)
-        h2[rel, :, 128 + ROPE :] = jnp.zeros((128, 128 - ROPE), BF16)
+        main = dot(by_z, full[:, COLS_Y:].astype(BF16)).astype(BF16)
+        rope = dk[:, LATENT:].astype(BF16)
+        low = dot(by_z_low, rope)
+        high = dot(by_z_high, rope)
+        side = jnp.concatenate([low, high], axis=1).astype(BF16)
+        for l in range(ZL):
+            h2[rel, l, 0:32, :] = main[l * 32 : l * 32 + 32, :]
+            h2[rel, l, 32:48, :] = side[l * 16 : l * 16 + 16, :]
+        return gain + jnp.sum(full * kr[rel, :, :LATENT].astype(F32), axis=0, keepdims=True)
 
     def pack(row, ref):
         for t in range(4):
             ref[t : t + 1, :] = row[:, t * 128 : (t + 1) * 128]
         ref[4:8, :] = jnp.zeros((4, 128), F32)
 
+    def y_rows(dy):
+        return pl.ds(pl.multiple_of(((y + dy) % Y) * 16, 16), 16)
+
+    def z_at(dz):
+        z = (zh * ZL + zl + dz) % (ZH * ZL)
+        return (z // ZL + ZH - zh) % ZH, z % ZL
+
+    for rel in (1, 2):
+        gain = key_part(rel, gain)
+    stage_z = [remote(h2.at[z_at(d)], h2_in.at[i], dz=d) for i, d in enumerate(Z_PEERS)]
+    for copy in stage_z[:Z_FAR]:
+        copy.start()
+    gain = key_part(0, gain)
+    stage_y = [remote(h1.at[:, y_rows(d), :], h1_in.at[i], dy=d) for i, d in enumerate(Y_PEERS)]
+    for copy in stage_y[:3]:
+        copy.start()
     pack(gain, ga)
     gain_a = [remote(ga, ga_in.at[i], dx=d, dc=c) for i, (d, c) in enumerate(X_PEERS)]
     for copy in gain_a:
         copy.start()
-
-    def y_rows(dy):
-        return pl.ds(pl.multiple_of(((y + dy) % Y) * 16, 16), 16)
-
-    def z_rows(dl):
-        return pl.ds(pl.multiple_of(((zl + dl) % ZL) * 32, 32), 32)
-
-    stage_y = [remote(h1.at[:, y_rows(d), :], h1_in.at[i], dy=d) for i, d in enumerate(Y_PEERS)]
-    stage_z = [
-        remote(h2.at[rel, z_rows(d), :], h2_in.at[i], dh=rel, dl=d)
-        for i, (rel, d) in enumerate(Z_PEERS)
-    ]
-    for i in range(len(Z_PEERS)):
-        stage_z[i].start()
-        if i < len(Y_PEERS):
-            stage_y[i].start()
+    for copy in stage_z[Z_FAR:] + stage_y[3:]:
+        copy.start()
 
     def query_part(cc):
         total = dot(kt[0], ds[cc, 0:128, :])
@@ -260,20 +274,19 @@
                 t1[rel, l, t * 4 : t * 4 + 4, :] = part[l * 4 : l * 4 + 4, t * 128 : (t + 1) * 128]
     h1b[...] = t1[...].astype(BF16)
     stage_yz = [
-        remote(h1b.at[rel, (zl + d) % ZL], h1b_in.at[i], dh=rel, dl=d)
-        for i, (rel, d) in enumerate(Z_PEERS)
+        remote(h1b.at[z_at(d)], h1b_in.at[i], dz=d) for i, d in enumerate(Z_PEERS)
     ]
     for copy in stage_yz:
         copy.start()
 
     for copy in stage_z:
         copy.wait_recv()
-    part = h2[0, z_rows(0), :].astype(F32)
+    part = h2[0, zl].astype(F32)
     for i in range(len(Z_PEERS)):
         part = part + h2_in[i].astype(F32)
     for yy in range(Y):
-        for t in range(2):
-            t2[yy, t * 4 : t * 4 + 4, :] = part[yy * 4 : yy * 4 + 4, t * 128 : (t + 1) * 128]
+        t2[yy, 0:4, :] = part[yy * 4 : yy * 4 + 4, :]
+        t2[yy, 4:8, :] = part[32 + (yy % 4) * 4 : 36 + (yy % 4) * 4, :]
     stage_zy = [remote(t2.at[(y + d) % Y], t2_in.at[i], dy=d) for i, d in enumerate(Y_PEERS)]
     for copy in stage_zy:
         copy.start()
@@ -284,7 +297,7 @@
     for i in range(len(Y_PEERS)):
         total = total + gb_in[i]
     gc[...] = total
-    gain_c = [remote(gc, gc_in.at[i], dh=rel, dl=d) for i, (rel, d) in enumerate(Z_PEERS)]
+    gain_c = [remote(gc, gc_in.at[i], dz=d) for i, d in enumerate(Z_PEERS)]
     for copy in gain_c:
         copy.start()
 
@@ -301,7 +314,7 @@
     for i in range(len(Y_PEERS)):
         part = part + t2_in[i]
     gk_ref[:, COLS_Y:LATENT] = part[0:4, :]
-    gk_ref[:, LATENT:] = part[4:8, :ROPE]
+    gk_ref[:, LATENT:] = jnp.where(y < Y // 2, part[4:8, :ROPE], part[4:8, ROPE:])
     for copy in gain_c:
         copy.wait_recv()
     total = gc[...]
@@ -311,29 +324,43 @@
 
     for copy in stores:
         copy.wait()
-    sent = list(first.values()) + second + [swap_q, swap_do, swap_stat] + swap_dq
+    sent = list(first.values()) + second[1] + second[2] + [swap_q, swap_do, swap_stat] + swap_dq
     sent += gain_a + gain_b + gain_c + stage_y + stage_z + stage_yz + stage_zy
     for copy in sent:
         copy.wait_send()
 
 
 N_COPIES = 4 + 12 + 3 + 2 + len(X_PEERS) + 3 * len(Y_PEERS) + 3 * len(Z_PEERS)
+
+
+def finish(gq_in, gk_in, gg_in, gq_out, gk_out, gg_out, sem):
+    copies = [
+        pltpu.make_async_copy(gq_in, gq_out, sem.at[0]),
+        pltpu.make_async_copy(gk_in, gk_out, sem.at[1]),
+        pltpu.make_async_copy(gg_in, gg_out, sem.at[2]),
+    ]
+    for copy in copies:
+        copy.start()
+    for copy in copies:
+        copy.wait()
 
 
 def body(queries, out_grad, latent_keys, kv_gain, query_groups):
     q_t = jnp.transpose(queries[0], (1, 2, 0))
     k_t = jnp.transpose(latent_keys[0], (1, 0))
     any_spec = pl.BlockSpec(memory_space=pl.ANY)
+    hbm_spec = pl.BlockSpec(memory_space=pltpu.HBM)
     vmem_spec = pl.BlockSpec(memory_space=pltpu.VMEM)
     ny, nz, nx = len(Y_PEERS), len(Z_PEERS), len(X_PEERS)
+    results = (
+        jax.ShapeDtypeStruct((4, WIDTH, 128), BF16),
+        jax.ShapeDtypeStruct((4, WIDTH), F32),
+        jax.ShapeDtypeStruct((4, 128), F32),
+    )
     gq, gk, gg = pl.pallas_call(
         kernel,
-        out_shape=(
-            jax.ShapeDtypeStruct((4, WIDTH, 128), BF16),
-            jax.ShapeDtypeStruct((4, WIDTH), F32),
-            jax.ShapeDtypeStruct((4, 128), F32),
-        ),
-        in_specs=[any_spec, any_spec, any_spec, vmem_spec, pl.BlockSpec(memory_space=pltpu.SMEM)],
+        out_shape=results,
+        in_specs=[hbm_spec, hbm_spec, hbm_spec, vmem_spec, pl.BlockSpec(memory_space=pltpu.SMEM)],
         out_specs=(any_spec, vmem_spec, vmem_spec),
         scratch_shapes=[
             pltpu.VMEM((4, WIDTH, 256), BF16),
@@ -349,9 +376,9 @@
             pltpu.VMEM((4, 8, 256), F32),
             pltpu.VMEM((4, 8, 256), F32),
             pltpu.VMEM((3, 128, COLS_Y), BF16),
-            pltpu.VMEM((3, 128, 256), BF16),
+            pltpu.VMEM((3, ZL, 48, 128), BF16),
             pltpu.VMEM((ny, 3, 16, COLS_Y), BF16),
-            pltpu.VMEM((nz, 32, 256), BF16),
+            pltpu.VMEM((nz, 48, 128), BF16),
             pltpu.VMEM((3, ZL, 16, 128), F32),
             pltpu.VMEM((3, ZL, 16, 128), BF16),
             pltpu.VMEM((nz, 16, 128), BF16),
@@ -371,13 +398,22 @@
             pltpu.SemaphoreType.DMA((N_COPIES,)),
         ],
         compiler_params=pltpu.CompilerParams(
-            collective_id=0, has_side_effects=True, vmem_limit_bytes=48 * 2**20
+            collective_id=0, has_side_effects=True, vmem_limit_bytes=60 * 2**20
         ),
         cost_estimate=pl.CostEstimate(
             flops=5 * 2 * 512 * 768 * 550, bytes_accessed=3 * 2**20, transcendentals=512 * 768
         ),
         name="mla_backward",
     )(q_t, out_grad[0], k_t, kv_gain.reshape(4, 128), query_groups)
+    gq, gk, gg = pl.pallas_call(
+        finish,
+        out_shape=results,
+        in_specs=[any_spec] * 3,
+        out_specs=(any_spec,) * 3,
+        scratch_shapes=[pltpu.SemaphoreType.DMA((3,))],
+        compiler_params=pltpu.CompilerParams(vmem_limit_bytes=60 * 2**20),
+        name="results",
+    )(gq, gk, gg)
     grad_queries = jnp.transpose(gq, (2, 0, 1))[None]
     return grad_queries, gk.reshape(1, 1, 4, WIDTH), gg.reshape(LATENT)
 

time: 59.7 us -> 73.5 us (1.23)
  Pallas kernels: 53.1 us -> 72.7 us
  local copies, waits for them, and re-layouts: 5.68 us -> 0 us
    pallas_call x1 -> x2, Pallas kernels: 53.1 us -> 72.7 us  [the longest x1 53.3 us: body(): pl.pallas_call(kernel, out_shape=results, in_specs=[hbm_spec, hbm_spec, h...]
    unnamed x13 -> x0, local copies, waits for them, and re-layouts: 5.68 us -> none
where the time goes in v2:
time: 73.5 us; the launch traced here: 73.3 us
  Pallas kernels  72.7 us (99%)
    pallas_call x1, Pallas kernels, body(): pl.pallas_call(kernel, out_shape=results, in_specs=[hbm_spec, hbm_spec, h...  53.3 us
    pallas_call x1, Pallas kernels, body(): pl.pallas_call(finish, out_shape=results, in_specs=[any_spec] * 3, out_sp...  19.4 us

profile of v2, /device:TPU:1, one launch (start us, length us, event | category | flops | bytes accessed | tf_op | source)
XLA Modules:
  0.0 73.3 jit_solution(8412099474006987846)
XLA Ops:
  0.6 53.3 %mla_backward.1 = (bf16[4,576,128]{2,1,0:T(8,128)(2,1)}, f32[4,576]{1,0:T(4,128)}, f32[4,128]{1,0:T(4,128)}) custom-call(bf16[4,576,128]{2,1,0:T(8,128)(2,1)} %bitcast.13, bf16[128,4,512]{2,1,0:T(4,128)(2,1)} %bitcast.15, bf16[576,128]{1,0:T(8,128)(2,1)} %bitcast.16, f32[4,128]{1,0:T(4,128)} %bitcast.18, s32[1,6]{1,0:T(1,128)} %groups_ref.1), custom_call_target="tpu_custom_call" | custom-call | flops 2162688000 | bytes 3145728 | tf_op jit(solution)/shard_map/mla_backward/pallas_call | solution.py:360
  54.0 19.4 %results.1 = (bf16[4,576,128]{2,1,0:T(8,128)(2,1)}, f32[4,576]{1,0:T(4,128)}, f32[4,128]{1,0:T(4,128)}) custom-call(bf16[4,576,128]{2,1,0:T(8,128)(2,1)} %get-tuple-element.9.gq_in, f32[4,576]{1,0:T(4,128)} %get-tuple-element.10.gk_in, f32[4,128]{1,0:T(4,128)} %get-tuple-element.11.gg_in), custom_call_target="tpu_custom_call" | custom-call | tf_op jit(solution)/shard_map/results/pallas_call | solution.py:408

commit v3 on v2

--- a/solution.py
+++ b/solution.py
@@ -37,7 +37,7 @@
     gq_hbm, gk_ref, gg_ref,
     qp, do_raw, do_f32, dop, kt, kr, st, dpt, ds, pw,
     stat, stat_in, h1, h2, h1_in, h2_in, t1, h1b, h1b_in, t2, t2_in,
-    ga, ga_in, gb, gb_in, gc, gc_in, dq, dq_in, gq,
+    ga, ga_in, gb, gb_in, gc, gc_in, dq, dq_in, dq_own, gq,
     local_sem, send_sem, recv_sem,
 ):
     x = lax.axis_index("dp")
@@ -76,9 +76,9 @@
         copy.start()
 
     barrier = pltpu.get_barrier_semaphore()
-    peers = [dict(dz=d) for d in Z_PEERS]
-    peers += [dict(dy=d) for d in Y_PEERS]
-    peers += [dict(dx=d, dc=c) for d, c in X_PEERS]
+    peers = [dict(dz=d) for d in (4, 8, 2, 10, 1, 11)]
+    peers += [dict(dy=d) for d in (2, 6, 1, 7)]
+    peers += [dict(dx=d) for d in (2, 1, 3)] + [dict(dc=1)]
     for peer in peers:
         pl.semaphore_signal(barrier, inc=1, device_id=device(**peer), device_id_type=MESH_ID)
     loads[0].wait()
@@ -249,18 +249,8 @@
     for copy in gain_b:
         copy.start()
 
-    stores = []
     for cc in range(2):
-        own = query_part(cc)
-        swap_dq[cc].wait_recv()
-        gq[cc] = (own + dq_in[cc]).astype(BF16)
-        for h in range(2):
-            store = pltpu.make_async_copy(
-                gq.at[cc, :, pl.ds(h * 128, 128)], gq_hbm.at[cc * 2 + h],
-                local_sem.at[6 + cc * 2 + h],
-            )
-            store.start()
-            stores.append(store)
+        dq_own[cc] = query_part(cc)
 
     t1[...] = jnp.zeros_like(t1)
     for copy in stage_y:
@@ -279,6 +269,16 @@
     for copy in stage_yz:
         copy.start()
 
+    for copy in gain_b:
+        copy.wait_recv()
+    total = gb[...]
+    for i in range(len(Y_PEERS)):
+        total = total + gb_in[i]
+    gc[...] = total
+    gain_c = [remote(gc, gc_in.at[i], dz=d) for i, d in enumerate(Z_PEERS)]
+    for copy in gain_c:
+        copy.start()
+
     for copy in stage_z:
         copy.wait_recv()
     part = h2[0, zl].astype(F32)
@@ -291,15 +291,17 @@
     for copy in stage_zy:
         copy.start()
 
-    for copy in gain_b:
-        copy.wait_recv()
-    total = gb[...]
-    for i in range(len(Y_PEERS)):
-        total = total + gb_in[i]
-    gc[...] = total
-    gain_c = [remote(gc, gc_in.at[i], dz=d) for i, d in enumerate(Z_PEERS)]
-    for copy in gain_c:
-        copy.start()
+    stores = []
+    for cc in range(2):
+        swap_dq[cc].wait_recv()
+        gq[cc] = (dq_own[cc] + dq_in[cc]).astype(BF16)
+        for h in range(2):
+            store = pltpu.make_async_copy(
+                gq.at[cc, :, pl.ds(h * 128, 128)], gq_hbm.at[cc * 2 + h],
+                local_sem.at[6 + cc * 2 + h],
+            )
+            store.start()
+            stores.append(store)
 
     for copy in stage_yz:
         copy.wait_recv()
@@ -333,15 +335,17 @@
 N_COPIES = 4 + 12 + 3 + 2 + len(X_PEERS) + 3 * len(Y_PEERS) + 3 * len(Z_PEERS)
 
 
-def finish(gq_in, gk_in, gg_in, gq_out, gk_out, gg_out, sem):
-    copies = [
-        pltpu.make_async_copy(gq_in, gq_out, sem.at[0]),
-        pltpu.make_async_copy(gk_in, gk_out, sem.at[1]),
-        pltpu.make_async_copy(gg_in, gg_out, sem.at[2]),
-    ]
-    for copy in copies:
-        copy.start()
-    for copy in copies:
+def finish(gq_in, gk_in, gg_in, gq_out, gk_out, gg_out, gq, gk, gg, in_sem, out_sem):
+    views = [(gq_in.at[h], gq.at[h], gq_out.at[h]) for h in range(4)]
+    views += [(gk_in, gk, gk_out), (gg_in, gg, gg_out)]
+    loads = [pltpu.make_async_copy(a, b, in_sem.at[i]) for i, (a, b, _) in enumerate(views)]
+    stores = [pltpu.make_async_copy(b, c, out_sem.at[i]) for i, (_, b, c) in enumerate(views)]
+    for copy in loads:
+        copy.start()
+    for load, store in zip(loads, stores):
+        load.wait()
+        store.start()
+    for copy in stores:
         copy.wait()
 
 
@@ -392,6 +396,7 @@
             pltpu.VMEM((nz, 8, 128), F32),
             pltpu.VMEM((2, WIDTH, 256), F32),
             pltpu.VMEM((2, WIDTH, 256), F32),
+            pltpu.VMEM((2, WIDTH, 256), F32),
             pltpu.VMEM((2, WIDTH, 256), BF16),
             pltpu.SemaphoreType.DMA((10,)),
             pltpu.SemaphoreType.DMA((N_COPIES,)),
@@ -410,7 +415,8 @@
         out_shape=results,
         in_specs=[any_spec] * 3,
         out_specs=(any_spec,) * 3,
-        scratch_shapes=[pltpu.SemaphoreType.DMA((3,))],
+        scratch_shapes=[pltpu.VMEM(r.shape, r.dtype) for r in results]
+        + [pltpu.SemaphoreType.DMA((6,)), pltpu.SemaphoreType.DMA((6,))],
         compiler_params=pltpu.CompilerParams(vmem_limit_bytes=60 * 2**20),
         name="results",
     )(gq, gk, gg)

time: 73.5 us -> 54.6 us (0.74)
  Pallas kernels: 72.7 us -> 53.8 us
    pallas_call x1, Pallas kernels: 19.4 us -> 1.89 us  [body(): pl.pallas_call(finish, out_shape=results, in_specs=[any_spec] * 3, out_sp...]
    pallas_call x1, Pallas kernels: 53.3 us -> 51.9 us  [body(): pl.pallas_call(kernel, out_shape=results, in_specs=[hbm_spec, hbm_spec, h...]
where the time goes in v3:
time: 54.6 us; the launch traced here: 54.4 us
  Pallas kernels  53.8 us (99%)
  between operations  0.64 us (1%)
    pallas_call x1, Pallas kernels, body(): pl.pallas_call(kernel, out_shape=results, in_specs=[hbm_spec, hbm_spec, h...  51.9 us
    pallas_call x1, Pallas kernels, body(): pl.pallas_call(finish, out_shape=results, in_specs=[any_spec] * 3, out_sp...  1.89 us

profile of v3, /device:TPU:1, one launch (start us, length us, event | category | flops | bytes accessed | tf_op | source)
XLA Modules:
  0.0 54.4 jit_solution(11680682909651920274)
XLA Ops:
  0.6 51.9 %mla_backward.1 = (bf16[4,576,128]{2,1,0:T(8,128)(2,1)}, f32[4,576]{1,0:T(4,128)}, f32[4,128]{1,0:T(4,128)}) custom-call(bf16[4,576,128]{2,1,0:T(8,128)(2,1)} %bitcast.13, bf16[128,4,512]{2,1,0:T(4,128)(2,1)} %bitcast.15, bf16[576,128]{1,0:T(8,128)(2,1)} %bitcast.16, f32[4,128]{1,0:T(4,128)} %bitcast.18, s32[1,6]{1,0:T(1,128)} %groups_ref.1), custom_call_target="tpu_custom_call" | custom-call | flops 2162688000 | bytes 3145728 | tf_op jit(solution)/shard_map/mla_backward/pallas_call | solution.py:364
  52.6 1.9 %results.1 = (bf16[4,576,128]{2,1,0:T(8,128)(2,1)}, f32[4,576]{1,0:T(4,128)}, f32[4,128]{1,0:T(4,128)}) custom-call(bf16[4,576,128]{2,1,0:T(8,128)(2,1)} %get-tuple-element.9.gq_in, f32[4,576]{1,0:T(4,128)} %get-tuple-element.10.gk_in, f32[4,128]{1,0:T(4,128)} %get-tuple-element.11.gg_in), custom_call_target="tpu_custom_call" | custom-call | tf_op jit(solution)/shard_map/results/pallas_call | solution.py:413

commit v4 on v3

--- a/solution.py
+++ b/solution.py
@@ -33,11 +33,11 @@
 
 
 def kernel(
-    q_hbm, do_hbm, kt_hbm, gain_ref, groups_ref,
-    gq_hbm, gk_ref, gg_ref,
+    q_hbm, do_hbm, kt_hbm, gain_hbm, groups_hbm,
+    gq_ref, gk_ref, gg_ref,
     qp, do_raw, do_f32, dop, kt, kr, st, dpt, ds, pw,
     stat, stat_in, h1, h2, h1_in, h2_in, t1, h1b, h1b_in, t2, t2_in,
-    ga, ga_in, gb, gb_in, gc, gc_in, dq, dq_in, dq_own, gq,
+    ga, ga_in, gb, gb_in, gc, gc_in, dq, dq_in, dq_own, gain_ref, groups_ref,
     local_sem, send_sem, recv_sem,
 ):
     x = lax.axis_index("dp")
@@ -72,8 +72,11 @@
                 q_hbm.at[h], qp.at[h // 2, :, pl.ds((h % 2) * 128, 128)], local_sem.at[2 + h]
             )
         )
-    for copy in loads:
-        copy.start()
+    tables = [
+        pltpu.make_async_copy(gain_hbm, gain_ref, local_sem.at[6]),
+        pltpu.make_async_copy(groups_hbm, groups_ref, local_sem.at[7]),
+    ]
+    loads[0].start()
 
     barrier = pltpu.get_barrier_semaphore()
     peers = [dict(dz=d) for d in (4, 8, 2, 10, 1, 11)]
@@ -81,6 +84,8 @@
     peers += [dict(dx=d) for d in (2, 1, 3)] + [dict(dc=1)]
     for peer in peers:
         pl.semaphore_signal(barrier, inc=1, device_id=device(**peer), device_id_type=MESH_ID)
+    for copy in loads[1:] + tables:
+        copy.start()
     loads[0].wait()
     pl.semaphore_wait(barrier, len(peers))
 
@@ -115,6 +120,8 @@
 
     swap_q.wait_recv()
     swap_do.wait_recv()
+    for copy in tables:
+        copy.wait()
 
     def keys_in(rel):
         for c in range(0, LATENT, 128):
@@ -126,14 +133,23 @@
     )
     group = (groups_ref[0, ctx], groups_ref[0, zh * CORES + 1 - core])
 
+    parts = {}
+
     def score(rel):
         base = ((zh + rel) % ZH) * CORES + core
+        rows = pl.ds(rel * 128, 128)
         keys = kr[rel]
         for cc in range(4):
             visible = diff <= (group[cc // 2] - base) * 128
-            s = dot(keys, qp[cc]) * SCALE
-            st[cc, pl.ds(rel * 128, 128), :] = jnp.where(visible, s, MASKED)
-            dpt[cc, pl.ds(rel * 128, 128), :] = dot(keys[:, :LATENT], dop[cc], NT)
+            s = jnp.where(visible, dot(keys, qp[cc]) * SCALE, MASKED)
+            dp = dot(keys[:, :LATENT], dop[cc], NT)
+            m = jnp.max(s, axis=0, keepdims=True)
+            p = jnp.where(visible, jnp.exp(s - m), 0.0)
+            st[cc, rows, :] = p
+            dpt[cc, rows, :] = dp
+            parts[rel, cc] = (
+                m, jnp.sum(p, axis=0, keepdims=True), jnp.sum(p * dp, axis=0, keepdims=True)
+            )
 
     keys_in(0)
     score(0)
@@ -144,18 +160,17 @@
         score(rel)
 
     for cc in range(4):
-        s = st[cc]
-        m = jnp.max(s, axis=0, keepdims=True)
-        p = jnp.where(s > 0.5 * MASKED, jnp.exp(s - m), 0.0)
-        st[cc] = p
+        m = jnp.maximum(jnp.maximum(parts[0, cc][0], parts[1, cc][0]), parts[2, cc][0])
+        e = [jnp.exp(parts[rel, cc][0] - m) for rel in range(3)]
         stat[cc, 0:1, :] = m
-        stat[cc, 1:2, :] = jnp.sum(p, axis=0, keepdims=True)
-        stat[cc, 2:3, :] = jnp.sum(p * dpt[cc], axis=0, keepdims=True)
+        stat[cc, 1:2, :] = sum(parts[rel, cc][1] * e[rel] for rel in range(3))
+        stat[cc, 2:3, :] = sum(parts[rel, cc][2] * e[rel] for rel in range(3))
         stat[cc, 3:8, :] = jnp.zeros((5, 256), F32)
     swap_stat = remote(stat, stat_in, dc=1)
     swap_stat.start()
     swap_stat.wait_recv()
 
+    both = []
     for cc in range(4):
         other = (cc + 2) % 4
         m0, l0, w0 = stat[cc, 0:1, :], stat[cc, 1:2, :], stat[cc, 2:3, :]
@@ -163,10 +178,15 @@
         m = jnp.maximum(m0, m1)
         e0, e1 = jnp.exp(m0 - m), jnp.exp(m1 - m)
         inv = 1.0 / (l0 * e0 + l1 * e1)
-        delta = (w0 * e0 + w1 * e1) * inv
-        w = st[cc] * (e0 * inv)
-        pw[cc] = w.astype(BF16)
-        ds[cc] = (w * (dpt[cc] - delta)).astype(BF16)
+        both.append((m, inv, (w0 * e0 + w1 * e1) * inv))
+
+    def weigh(rel):
+        rows = pl.ds(rel * 128, 128)
+        for cc in range(4):
+            m, inv, delta = both[cc]
+            w = st[cc, rows, :] * (jnp.exp(parts[rel, cc][0] - m) * inv)
+            pw[cc, rows, :] = w.astype(BF16)
+            ds[cc, rows, :] = (w * (dpt[cc, rows, :] - delta)).astype(BF16)
 
     def picks(rows, wanted):
         out_row = lax.broadcasted_iota(jnp.int32, (rows, 128), 0)
@@ -178,25 +198,32 @@
     by_z_high = picks(64, lambda o: (((o & 15) >> 2) + 4) * 16 + (o >> 4) * 4 + (o & 3))
     gain = jnp.zeros((1, LATENT), F32)
 
-    def key_part(rel, gain):
-        rows = pl.ds(rel * 128, 128)
+    def key_part(start, groups, gain):
+        for rel in range(start, start + groups):
+            weigh(rel)
+        rows = pl.ds(start * 128, groups * 128)
         dk = dot(ds[0, rows, :], qp[0], NT)
         dv = dot(pw[0, rows, :], dop[0])
         for cc in range(1, 4):
             dk = dk + dot(ds[cc, rows, :], qp[cc], NT)
             dv = dv + dot(pw[cc, rows, :], dop[cc])
         dk = dk * SCALE
-        full = dk[:, :LATENT] + dv
-        h1[rel] = full[:, :COLS_Y].astype(BF16)
-        main = dot(by_z, full[:, COLS_Y:].astype(BF16)).astype(BF16)
-        rope = dk[:, LATENT:].astype(BF16)
-        low = dot(by_z_low, rope)
-        high = dot(by_z_high, rope)
-        side = jnp.concatenate([low, high], axis=1).astype(BF16)
-        for l in range(ZL):
-            h2[rel, l, 0:32, :] = main[l * 32 : l * 32 + 32, :]
-            h2[rel, l, 32:48, :] = side[l * 16 : l * 16 + 16, :]
-        return gain + jnp.sum(full * kr[rel, :, :LATENT].astype(F32), axis=0, keepdims=True)
+        dv = dk[:, :LATENT] + dv
+        for g in range(groups):
+            rel = start + g
+            full = dv[g * 128 : g * 128 + 128]
+            h1[rel] = full[:, :COLS_Y].astype(BF16)
+            main = dot(by_z, full[:, COLS_Y:].astype(BF16)).astype(BF16)
+            rope = dk[g * 128 : g * 128 + 128, LATENT:].astype(BF16)
+            low = dot(by_z_low, rope)
+            high = dot(by_z_high, rope)
+            side = jnp.concatenate([low, high], axis=1).astype(BF16)
+            for l in range(ZL):
+                h2[rel, l, 0:32, :] = main[l * 32 : l * 32 + 32, :]
+                h2[rel, l, 32:48, :] = side[l * 16 : l * 16 + 16, :]
+            keys = kr[rel, :, :LATENT].astype(F32)
+            gain = gain + jnp.sum(full * keys, axis=0, keepdims=True)
+        return gain
 
     def pack(row, ref):
         for t in range(4):
@@ -210,21 +237,23 @@
         z = (zh * ZL + zl + dz) % (ZH * ZL)
         return (z // ZL + ZH - zh) % ZH, z % ZL
 
-    for rel in (1, 2):
-        gain = key_part(rel, gain)
+    gain = key_part(1, 2, gain)
     stage_z = [remote(h2.at[z_at(d)], h2_in.at[i], dz=d) for i, d in enumerate(Z_PEERS)]
-    for copy in stage_z[:Z_FAR]:
-        copy.start()
-    gain = key_part(0, gain)
-    stage_y = [remote(h1.at[:, y_rows(d), :], h1_in.at[i], dy=d) for i, d in enumerate(Y_PEERS)]
-    for copy in stage_y[:3]:
-        copy.start()
+    stage_y = [
+        remote(h1.at[pl.ds(1, 2), y_rows(d), :], h1_in.at[i, pl.ds(1, 2)], dy=d)
+        for i, d in enumerate(Y_PEERS)
+    ]
+    for i, copy in enumerate(stage_y):
+        copy.start()
+        if i < Z_FAR:
+            stage_z[i].start()
+    gain = key_part(0, 1, gain)
+    last_y = [remote(h1.at[0, y_rows(d), :], h1_in.at[i, 0], dy=d) for i, d in enumerate(Y_PEERS)]
     pack(gain, ga)
     gain_a = [remote(ga, ga_in.at[i], dx=d, dc=c) for i, (d, c) in enumerate(X_PEERS)]
-    for copy in gain_a:
-        copy.start()
-    for copy in stage_z[Z_FAR:] + stage_y[3:]:
-        copy.start()
+    for copy in last_y + gain_a + stage_z[Z_FAR:]:
+        copy.start()
+    stage_y = stage_y + last_y
 
     def query_part(cc):
         total = dot(kt[0], ds[cc, 0:128, :])
@@ -291,17 +320,11 @@
     for copy in stage_zy:
         copy.start()
 
-    stores = []
     for cc in range(2):
         swap_dq[cc].wait_recv()
-        gq[cc] = (dq_own[cc] + dq_in[cc]).astype(BF16)
-        for h in range(2):
-            store = pltpu.make_async_copy(
-                gq.at[cc, :, pl.ds(h * 128, 128)], gq_hbm.at[cc * 2 + h],
-                local_sem.at[6 + cc * 2 + h],
-            )
-            store.start()
-            stores.append(store)
+        full = (dq_own[cc] + dq_in[cc]).astype(BF16)
+        gq_ref[cc * 2] = full[:, :128]
+        gq_ref[cc * 2 + 1] = full[:, 128:]
 
     for copy in stage_yz:
         copy.wait_recv()
@@ -324,28 +347,21 @@
         total = total + gc_in[i]
     gg_ref[...] = total[0:4, :] / gain_ref[...]
 
-    for copy in stores:
-        copy.wait()
     sent = list(first.values()) + second[1] + second[2] + [swap_q, swap_do, swap_stat] + swap_dq
     sent += gain_a + gain_b + gain_c + stage_y + stage_z + stage_yz + stage_zy
     for copy in sent:
         copy.wait_send()
 
 
-N_COPIES = 4 + 12 + 3 + 2 + len(X_PEERS) + 3 * len(Y_PEERS) + 3 * len(Z_PEERS)
-
-
-def finish(gq_in, gk_in, gg_in, gq_out, gk_out, gg_out, gq, gk, gg, in_sem, out_sem):
-    views = [(gq_in.at[h], gq.at[h], gq_out.at[h]) for h in range(4)]
-    views += [(gk_in, gk, gk_out), (gg_in, gg, gg_out)]
-    loads = [pltpu.make_async_copy(a, b, in_sem.at[i]) for i, (a, b, _) in enumerate(views)]
-    stores = [pltpu.make_async_copy(b, c, out_sem.at[i]) for i, (_, b, c) in enumerate(views)]
-    for copy in loads:
-        copy.start()
-    for load, store in zip(loads, stores):
-        load.wait()
-        store.start()
-    for copy in stores:
+N_COPIES = 4 + 12 + 3 + 2 + len(X_PEERS) + 4 * len(Y_PEERS) + 3 * len(Z_PEERS)
+
+
+def finish(gq_in, gk_in, gg_in, gq_out, gk_out, gg_out, sem):
+    pairs = [(gk_in, gk_out), (gg_in, gg_out)] + [(gq_in.at[h], gq_out.at[h]) for h in range(4)]
+    copies = [pltpu.make_async_copy(a, b, sem.at[i]) for i, (a, b) in enumerate(pairs)]
+    for copy in copies:
+        copy.start()
+    for copy in copies:
         copy.wait()
 
 
@@ -353,9 +369,10 @@
     q_t = jnp.transpose(queries[0], (1, 2, 0))
     k_t = jnp.transpose(latent_keys[0], (1, 0))
     any_spec = pl.BlockSpec(memory_space=pl.ANY)
-    hbm_spec = pl.BlockSpec(memory_space=pltpu.HBM)
     vmem_spec = pl.BlockSpec(memory_space=pltpu.VMEM)
     ny, nz, nx = len(Y_PEERS), len(Z_PEERS), len(X_PEERS)
+    given = (q_t, out_grad[0], k_t, kv_gain.reshape(4, 128), query_groups)
+    given = [pltpu.with_memory_space_constraint(a, pltpu.HBM) for a in given]
     results = (
         jax.ShapeDtypeStruct((4, WIDTH, 128), BF16),
         jax.ShapeDtypeStruct((4, WIDTH), F32),
@@ -364,8 +381,8 @@
     gq, gk, gg = pl.pallas_call(
         kernel,
         out_shape=results,
-        in_specs=[hbm_spec, hbm_spec, hbm_spec, vmem_spec, pl.BlockSpec(memory_space=pltpu.SMEM)],
-        out_specs=(any_spec, vmem_spec, vmem_spec),
+        in_specs=[any_spec] * 5,
+        out_specs=(vmem_spec,) * 3,
         scratch_shapes=[
             pltpu.VMEM((4, WIDTH, 256), BF16),
             pltpu.VMEM((128, 4, LATENT), BF16),
@@ -397,27 +414,26 @@
             pltpu.VMEM((2, WIDTH, 256), F32),
             pltpu.VMEM((2, WIDTH, 256), F32),
             pltpu.VMEM((2, WIDTH, 256), F32),
-            pltpu.VMEM((2, WIDTH, 256), BF16),
-            pltpu.SemaphoreType.DMA((10,)),
+            pltpu.VMEM((4, 128), F32),
+            pltpu.SMEM((1, 6), jnp.int32),
+            pltpu.SemaphoreType.DMA((8,)),
             pltpu.SemaphoreType.DMA((N_COPIES,)),
             pltpu.SemaphoreType.DMA((N_COPIES,)),
         ],
         compiler_params=pltpu.CompilerParams(
-            collective_id=0, has_side_effects=True, vmem_limit_bytes=60 * 2**20
+            collective_id=0, has_side_effects=True, vmem_limit_bytes=48 * 2**20
         ),
         cost_estimate=pl.CostEstimate(
             flops=5 * 2 * 512 * 768 * 550, bytes_accessed=3 * 2**20, transcendentals=512 * 768
         ),
         name="mla_backward",
-    )(q_t, out_grad[0], k_t, kv_gain.reshape(4, 128), query_groups)
+    )(*given)
     gq, gk, gg = pl.pallas_call(
         finish,
         out_shape=results,
         in_specs=[any_spec] * 3,
         out_specs=(any_spec,) * 3,
-        scratch_shapes=[pltpu.VMEM(r.shape, r.dtype) for r in results]
-        + [pltpu.SemaphoreType.DMA((6,)), pltpu.SemaphoreType.DMA((6,))],
-        compiler_params=pltpu.CompilerParams(vmem_limit_bytes=60 * 2**20),
+        scratch_shapes=[pltpu.SemaphoreType.DMA((6,))],
         name="results",
     )(gq, gk, gg)
     grad_queries = jnp.transpose(gq, (2, 0, 1))[None]

time: 54.6 us -> 72.3 us (1.32)
  Pallas kernels: 53.8 us -> 69.5 us
  local copies, waits for them, and re-layouts: 0 us -> 1.98 us
    pallas_call x1, Pallas kernels: 1.89 us -> 19.4 us  [body(): pl.pallas_call(finish, out_shape=results, in_specs=[any_spec] * 3, out_sp...]
    unnamed x0 -> x6, local copies, waits for them, and re-layouts: none -> 1.98 us
    pallas_call x1, Pallas kernels: 51.9 us -> 50.1 us  [body(): pl.pallas_call(kernel, out_shape=results, in_specs=[any_spec] * 5, out_sp...]
where the time goes in v4:
time: 72.3 us; the launch traced here: 72.1 us
  Pallas kernels  69.5 us (96%)
  local copies, waits for them, and re-layouts  1.98 us (3%)
    pallas_call x1, Pallas kernels, body(): pl.pallas_call(kernel, out_shape=results, in_specs=[any_spec] * 5, out_sp...  50.1 us
    pallas_call x1, Pallas kernels, body(): pl.pallas_call(finish, out_shape=results, in_specs=[any_spec] * 3, out_sp...  19.4 us
    unnamed x6, local copies, waits for them, and re-layouts  1.98 us

profile of v4, /device:TPU:1, one launch (start us, length us, event | category | flops | bytes accessed | tf_op | source)
XLA Modules:
  0.0 72.1 jit_solution(17260542062965798674)
XLA Ops:
  0.6 50.1 %mla_backward.1 = (bf16[4,576,128]{2,1,0:T(8,128)(2,1)S(1)}, f32[4,576]{1,0:T(4,128)S(1)}, f32[4,128]{1,0:T(4,128)S(1)}) custom-call(bf16[4,576,128]{2,1,0:T(8,128)(2,1)} %bitcast.13, bf16[128,4,512]{2,1,0:T(4,128)(2,1)} %bitcast.15, bf16[576,128]{1,0:T(8,128)(2,1)} %bitcast.16, f32[4,128]{1,0:T(4,128)} %bitcast.18, s32[1,6]{1,0:T(1,128)} %groups_hbm.1), custom_call_target="tpu_custom_call" | custom-call | flops 2162688000 | bytes 3145728 | tf_op jit(solution)/shard_map/mla_backward/pallas_call | solution.py:381
  50.7 0.0 copy-start
  50.7 0.8 %copy-done = bf16[4,576,128]{2,1,0:T(8,128)(2,1)} copy-done((bf16[4,576,128]{2,1,0:T(8,128)(2,1)}, bf16[4,576,128]{2,1,0:T(8,128)(2,1)S(1)}, u32[]{:S(2)}) %copy-start) | copy-done | bytes 589848
  51.6 0.0 copy-start.1
  51.6 0.6 copy-done.1
  52.2 0.0 copy-start.2
  52.2 0.6 copy-done.2
  52.7 19.4 %results.1 = (bf16[4,576,128]{2,1,0:T(8,128)(2,1)}, f32[4,576]{1,0:T(4,128)}, f32[4,128]{1,0:T(4,128)}) custom-call(bf16[4,576,128]{2,1,0:T(8,128)(2,1)} %copy-done, f32[4,576]{1,0:T(4,128)} %copy-done.1, f32[4,128]{1,0:T(4,128)} %copy-done.2), custom_call_target="tpu_custom_call" | custom-call | tf_op jit(solution)/shard_map/results/pallas_call | solution.py:431
Async XLA Ops:
  50.7 0.8 %copy-start = (bf16[4,576,128]{2,1,0:T(8,128)(2,1)}, bf16[4,576,128]{2,1,0:T(8,128)(2,1)S(1)}, u32[]{:S(2)}) copy-start(bf16[4,576,128]{2,1,0:T(8,128)(2,1)S(1)} %get-tuple-element.9.gq_in) | copy-start | bytes 1769476
  51.6 0.6 copy-start.1
  52.2 0.6 copy-start.2

commit v5 on v4

--- a/solution.py
+++ b/solution.py
@@ -36,7 +36,7 @@
     q_hbm, do_hbm, kt_hbm, gain_hbm, groups_hbm,
     gq_ref, gk_ref, gg_ref,
     qp, do_raw, do_f32, dop, kt, kr, st, dpt, ds, pw,
-    stat, stat_in, h1, h2, h1_in, h2_in, t1, h1b, h1b_in, t2, t2_in,
+    stat, stat_in, h1, h2, h3, h1_in, h2_in, h3_in, t1, h1b, h1b_in, t2, t2b, t2_in,
     ga, ga_in, gb, gb_in, gc, gc_in, dq, dq_in, dq_own, gain_ref, groups_ref,
     local_sem, send_sem, recv_sem,
 ):
@@ -46,8 +46,8 @@
     zh, core = ctx // CORES, ctx % CORES
     y, zl = exp // ZL, exp % ZL
 
-    def device(dx=0, dy=0, dz=0, dc=0):
-        z = (zh * ZL + zl + dz) % (ZH * ZL)
+    def device(dx=0, dy=0, dz=0, dl=0, dc=0):
+        z = (zh * ZL + (zl + dl) % ZL + dz) % (ZH * ZL)
         return (
             (x + dx) % X,
             (z // ZL) * CORES + (core + dc) % CORES,
@@ -91,8 +91,8 @@
 
     p0 = (y % 4) * QUARTER
     first = {}
-    for rel in (1, 2):
-        for at, (off, rows) in enumerate(PIECES):
+    for at, (off, rows) in enumerate(PIECES):
+        for rel in (1, 2):
             part = pl.ds(pl.multiple_of(p0 + off, 16), rows)
             first[rel, at] = remote(kt.at[0, part], kt.at[rel, part], dz=(ZH - rel) * ZL)
             first[rel, at].start()
@@ -108,15 +108,15 @@
     swap_do = remote(dop.at[pl.ds(0, 2)], dop.at[pl.ds(2, 2)], dc=1)
     swap_do.start()
 
-    second = {1: [], 2: []}
-    for rel in (1, 2):
-        for at, (off, rows) in enumerate(PIECES):
+    second = []
+    for at, (off, rows) in enumerate(PIECES):
+        for rel in (1, 2):
             first[rel, at].wait_recv()
             part = pl.ds(pl.multiple_of(p0 + off, 16), rows)
             for dy in (1, Y - 1, 2 if at == 0 else Y - 2):
                 copy = remote(kt.at[rel, part], kt.at[rel, part], dy=dy)
                 copy.start()
-                second[rel].append(copy)
+                second.append(copy)
 
     swap_q.wait_recv()
     swap_do.wait_recv()
@@ -135,29 +135,33 @@
 
     parts = {}
 
-    def score(rel):
-        base = ((zh + rel) % ZH) * CORES + core
-        rows = pl.ds(rel * 128, 128)
-        keys = kr[rel]
+    def score(start, groups):
+        first_row = start * 128
+        keys = kr[start : start + groups].reshape(groups * 128, WIDTH)
         for cc in range(4):
-            visible = diff <= (group[cc // 2] - base) * 128
-            s = jnp.where(visible, dot(keys, qp[cc]) * SCALE, MASKED)
-            dp = dot(keys[:, :LATENT], dop[cc], NT)
-            m = jnp.max(s, axis=0, keepdims=True)
-            p = jnp.where(visible, jnp.exp(s - m), 0.0)
-            st[cc, rows, :] = p
-            dpt[cc, rows, :] = dp
-            parts[rel, cc] = (
-                m, jnp.sum(p, axis=0, keepdims=True), jnp.sum(p * dp, axis=0, keepdims=True)
-            )
+            raw = dot(keys, qp[cc]) * SCALE
+            grad = dot(keys[:, :LATENT], dop[cc], NT)
+            dpt[cc, first_row : first_row + groups * 128, :] = grad
+            for g in range(groups):
+                rel = start + g
+                base = ((zh + rel) % ZH) * CORES + core
+                visible = diff <= (group[cc // 2] - base) * 128
+                s = jnp.where(visible, raw[g * 128 : g * 128 + 128], MASKED)
+                dp = grad[g * 128 : g * 128 + 128]
+                m = jnp.max(s, axis=0, keepdims=True)
+                p = jnp.where(visible, jnp.exp(s - m), 0.0)
+                st[cc, rel * 128 : rel * 128 + 128, :] = p
+                parts[rel, cc] = (
+                    m, jnp.sum(p, axis=0, keepdims=True), jnp.sum(p * dp, axis=0, keepdims=True)
+                )
 
     keys_in(0)
-    score(0)
+    score(0, 1)
+    for copy in second:
+        copy.wait_recv()
     for rel in (1, 2):
-        for copy in second[rel]:
-            copy.wait_recv()
         keys_in(rel)
-        score(rel)
+    score(1, 2)
 
     for cc in range(4):
         m = jnp.maximum(jnp.maximum(parts[0, cc][0], parts[1, cc][0]), parts[2, cc][0])
@@ -221,6 +225,11 @@
             for l in range(ZL):
                 h2[rel, l, 0:32, :] = main[l * 32 : l * 32 + 32, :]
                 h2[rel, l, 32:48, :] = side[l * 16 : l * 16 + 16, :]
+            if rel == 0:
+                for t in (1, 2):
+                    near = dot(by_z, h1[0, :, t * 128 : t * 128 + 128]).astype(BF16)
+                    for l in range(ZL):
+                        h3[l, t * 32 - 32 : t * 32, :] = near[l * 32 : l * 32 + 32, :]
             keys = kr[rel, :, :LATENT].astype(F32)
             gain = gain + jnp.sum(full * keys, axis=0, keepdims=True)
         return gain
@@ -248,10 +257,14 @@
         if i < Z_FAR:
             stage_z[i].start()
     gain = key_part(0, 1, gain)
-    last_y = [remote(h1.at[0, y_rows(d), :], h1_in.at[i, 0], dy=d) for i, d in enumerate(Y_PEERS)]
+    stage_l = [remote(h3.at[(zl + d) % ZL], h3_in.at[d - 1], dl=d) for d in (1, 2, 3)]
+    last_y = [
+        remote(h1.at[0, y_rows(d), pl.ds(0, 128)], h1_in.at[i, 0, :, pl.ds(0, 128)], dy=d)
+        for i, d in enumerate(Y_PEERS)
+    ]
     pack(gain, ga)
     gain_a = [remote(ga, ga_in.at[i], dx=d, dc=c) for i, (d, c) in enumerate(X_PEERS)]
-    for copy in last_y + gain_a + stage_z[Z_FAR:]:
+    for copy in stage_z[Z_FAR:] + stage_l + last_y + gain_a:
         copy.start()
     stage_y = stage_y + last_y
 
@@ -285,11 +298,12 @@
     for copy in stage_y:
         copy.wait_recv()
     for rel in range(3):
-        part = h1[rel, y_rows(0), :].astype(F32)
+        tiles = 3 if rel else 1
+        part = h1[rel, y_rows(0), : tiles * 128].astype(F32)
         for i in range(len(Y_PEERS)):
-            part = part + h1_in[i, rel].astype(F32)
+            part = part + h1_in[i, rel, :, : tiles * 128].astype(F32)
         for l in range(ZL):
-            for t in range(3):
+            for t in range(tiles):
                 t1[rel, l, t * 4 : t * 4 + 4, :] = part[l * 4 : l * 4 + 4, t * 128 : (t + 1) * 128]
     h1b[...] = t1[...].astype(BF16)
     stage_yz = [
@@ -308,15 +322,21 @@
     for copy in gain_c:
         copy.start()
 
-    for copy in stage_z:
+    for copy in stage_z + stage_l:
         copy.wait_recv()
     part = h2[0, zl].astype(F32)
     for i in range(len(Z_PEERS)):
         part = part + h2_in[i].astype(F32)
+    near = h3[zl].astype(F32)
+    for i in range(ZL - 1):
+        near = near + h3_in[i].astype(F32)
     for yy in range(Y):
         t2[yy, 0:4, :] = part[yy * 4 : yy * 4 + 4, :]
         t2[yy, 4:8, :] = part[32 + (yy % 4) * 4 : 36 + (yy % 4) * 4, :]
-    stage_zy = [remote(t2.at[(y + d) % Y], t2_in.at[i], dy=d) for i, d in enumerate(Y_PEERS)]
+        t2[yy, 8:12, :] = near[yy * 4 : yy * 4 + 4, :]
+        t2[yy, 12:16, :] = near[32 + yy * 4 : 36 + yy * 4, :]
+    t2b[...] = t2[...].astype(BF16)
+    stage_zy = [remote(t2b.at[(y + d) % Y], t2_in.at[i], dy=d) for i, d in enumerate(Y_PEERS)]
     for copy in stage_zy:
         copy.start()
 
@@ -326,20 +346,21 @@
         gq_ref[cc * 2] = full[:, :128]
         gq_ref[cc * 2 + 1] = full[:, 128:]
 
+    for copy in stage_zy:
+        copy.wait_recv()
+    late = t2[y]
+    for i in range(len(Y_PEERS)):
+        late = late + t2_in[i].astype(F32)
+    gk_ref[:, COLS_Y:LATENT] = late[0:4, :]
+    gk_ref[:, LATENT:] = jnp.where(y < Y // 2, late[4:8, :ROPE], late[4:8, ROPE:])
     for copy in stage_yz:
         copy.wait_recv()
     part = t1[0, zl]
     for i in range(len(Z_PEERS)):
         part = part + h1b_in[i].astype(F32)
-    for t in range(3):
-        gk_ref[:, t * 128 : (t + 1) * 128] = part[t * 4 : t * 4 + 4, :]
-    for copy in stage_zy:
-        copy.wait_recv()
-    part = t2[y]
-    for i in range(len(Y_PEERS)):
-        part = part + t2_in[i]
-    gk_ref[:, COLS_Y:LATENT] = part[0:4, :]
-    gk_ref[:, LATENT:] = jnp.where(y < Y // 2, part[4:8, :ROPE], part[4:8, ROPE:])
+    gk_ref[:, 0:128] = part[0:4, :]
+    gk_ref[:, 128:256] = part[4:8, :] + late[8:12, :]
+    gk_ref[:, 256:COLS_Y] = part[8:12, :] + late[12:16, :]
     for copy in gain_c:
         copy.wait_recv()
     total = gc[...]
@@ -347,13 +368,13 @@
         total = total + gc_in[i]
     gg_ref[...] = total[0:4, :] / gain_ref[...]
 
-    sent = list(first.values()) + second[1] + second[2] + [swap_q, swap_do, swap_stat] + swap_dq
-    sent += gain_a + gain_b + gain_c + stage_y + stage_z + stage_yz + stage_zy
+    sent = list(first.values()) + second + [swap_q, swap_do, swap_stat] + swap_dq
+    sent += gain_a + gain_b + gain_c + stage_y + stage_z + stage_l + stage_yz + stage_zy
     for copy in sent:
         copy.wait_send()
 
 
-N_COPIES = 4 + 12 + 3 + 2 + len(X_PEERS) + 4 * len(Y_PEERS) + 3 * len(Z_PEERS)
+N_COPIES = 4 + 12 + 3 + 2 + len(X_PEERS) + 4 * len(Y_PEERS) + 3 * len(Z_PEERS) + 3
 
 
 def finish(gq_in, gk_in, gg_in, gq_out, gk_out, gg_out, sem):
@@ -398,13 +419,16 @@
             pltpu.VMEM((4, 8, 256), F32),
             pltpu.VMEM((3, 128, COLS_Y), BF16),
             pltpu.VMEM((3, ZL, 48, 128), BF16),
+            pltpu.VMEM((ZL, 64, 128), BF16),
             pltpu.VMEM((ny, 3, 16, COLS_Y), BF16),
             pltpu.VMEM((nz, 48, 128), BF16),
+            pltpu.VMEM((ZL - 1, 64, 128), BF16),
             pltpu.VMEM((3, ZL, 16, 128), F32),
             pltpu.VMEM((3, ZL, 16, 128), BF16),
             pltpu.VMEM((nz, 16, 128), BF16),
-            pltpu.VMEM((Y, 8, 128), F32),
-            pltpu.VMEM((ny, 8, 128), F32),
+            pltpu.VMEM((Y, 16, 128), F32),
+            pltpu.VMEM((Y, 16, 128), BF16),
+            pltpu.VMEM((ny, 16, 128), BF16),
             pltpu.VMEM((8, 128), F32),
             pltpu.VMEM((nx, 8, 128), F32),
             pltpu.VMEM((8, 128), F32),
@@ -434,8 +458,9 @@
         in_specs=[any_spec] * 3,
         out_specs=(any_spec,) * 3,
         scratch_shapes=[pltpu.SemaphoreType.DMA((6,))],
+        compiler_params=pltpu.CompilerParams(vmem_limit_bytes=2**20),
         name="results",
-    )(gq, gk, gg)
+    )(*(pltpu.with_memory_space_constraint(a, pltpu.VMEM) for a in (gq, gk, gg)))
     grad_queries = jnp.transpose(gq, (2, 0, 1))[None]
     return grad_queries, gk.reshape(1, 1, 4, WIDTH), gg.reshape(LATENT)
 

time: 72.3 us -> 50 us (0.69)
  Pallas kernels: 69.5 us -> 49.3 us
  local copies, waits for them, and re-layouts: 1.98 us -> 0 us
    pallas_call x1, Pallas kernels: 19.4 us -> 0.87 us  [body(): pl.pallas_call(finish, out_shape=results, in_specs=[any_spec] * 3, out_sp...]
    unnamed x6 -> x0, local copies, waits for them, and re-layouts: 1.98 us -> none
    pallas_call x1, Pallas kernels: 50.1 us -> 48.4 us  [body(): pl.pallas_call(kernel, out_shape=results, in_specs=[any_spec] * 5, out_sp...]
where the time goes in v5:
time: 50 us; the launch traced here: 49.9 us
  Pallas kernels  49.3 us (99%)
  between operations  0.64 us (1%)
    pallas_call x1, Pallas kernels, body(): pl.pallas_call(kernel, out_shape=results, in_specs=[any_spec] * 5, out_sp...  48.4 us

profile of v5, /device:TPU:1, one launch (start us, length us, event | category | flops | bytes accessed | tf_op | source)
XLA Modules:
  0.0 49.9 jit_solution(16970517888103098414)
XLA Ops:
  0.6 48.4 %mla_backward.1 = (bf16[4,576,128]{2,1,0:T(8,128)(2,1)S(1)}, f32[4,576]{1,0:T(4,128)S(1)}, f32[4,128]{1,0:T(4,128)S(1)}) custom-call(bf16[4,576,128]{2,1,0:T(8,128)(2,1)} %bitcast.13, bf16[128,4,512]{2,1,0:T(4,128)(2,1)} %bitcast.15, bf16[576,128]{1,0:T(8,128)(2,1)} %bitcast.16, f32[4,128]{1,0:T(4,128)} %bitcast.18, s32[1,6]{1,0:T(1,128)} %groups_hbm.1), custom_call_target="tpu_custom_call" | custom-call | flops 2162688000 | bytes 3145728 | tf_op jit(solution)/shard_map/mla_backward/pallas_call | solution.py:402
  49.0 0.9 %results.1 = (bf16[4,576,128]{2,1,0:T(8,128)(2,1)}, f32[4,576]{1,0:T(4,128)}, f32[4,128]{1,0:T(4,128)}) custom-call(bf16[4,576,128]{2,1,0:T(8,128)(2,1)S(1)} %get-tuple-element.9.gq_in, f32[4,576]{1,0:T(4,128)S(1)} %get-tuple-element.10.gk_in, f32[4,128]{1,0:T(4,128)S(1)} %get-tuple-element.11.gg_in), custom_call_target="tpu_custom_call" | custom-call | tf_op jit(solution)/shard_map/results/pallas_call | solution.py:455

commit v6 on v5

--- a/solution.py
+++ b/solution.py
@@ -22,10 +22,26 @@
 Y_PEERS = (4, 3, 5, 2, 6, 1, 7)
 Z_PEERS = (6, 5, 7, 4, 8, 3, 9, 2, 10, 1, 11)
 Z_FAR = 5
+OTHER_GROUPS = tuple((rel, d) for rel in (1, 2) for d in range(ZL))
 X_PEERS = ((0, 1), (1, 0), (3, 0), (2, 0), (1, 1), (3, 1), (2, 1))
 COLS_Y = 384
 NT = (((1,), (1,)), ((), ()))
 NN = (((1,), (0,)), ((), ()))
+
+
+class Group:
+    def __init__(self, copies, sent, received):
+        self.copies, self.sent, self.received = copies, sent, received
+
+    def start(self):
+        for copy in self.copies:
+            copy.start()
+
+    def wait_send(self):
+        self.sent.wait()
+
+    def wait_recv(self):
+        self.received.wait()
 
 
 def dot(a, b, dims=NN):
@@ -56,12 +72,23 @@
 
     count = [0]
 
-    def remote(src, dst, **where):
-        i = count[0]
+    def take():
         count[0] += 1
+        return count[0] - 1
+
+    def remote(src, dst, at=None, **where):
+        i = take() if at is None else at
         return pltpu.make_async_remote_copy(
             src_ref=src, dst_ref=dst, send_sem=send_sem.at[i], recv_sem=recv_sem.at[i],
             device_id=device(**where), device_id_type=MESH_ID,
+        )
+
+    def together(whole, moves):
+        i = take()
+        return Group(
+            [remote(src, dst, at=i, **where) for src, dst, where in moves],
+            pltpu.make_async_copy(whole, whole, send_sem.at[i]),
+            pltpu.make_async_copy(whole, whole, recv_sem.at[i]),
         )
 
     loads = [pltpu.make_async_copy(kt_hbm, kt.at[0], local_sem.at[0])]
@@ -108,15 +135,19 @@
     swap_do = remote(dop.at[pl.ds(0, 2)], dop.at[pl.ds(2, 2)], dc=1)
     swap_do.start()
 
-    second = []
+    moves = []
     for at, (off, rows) in enumerate(PIECES):
         for rel in (1, 2):
-            first[rel, at].wait_recv()
             part = pl.ds(pl.multiple_of(p0 + off, 16), rows)
             for dy in (1, Y - 1, 2 if at == 0 else Y - 2):
-                copy = remote(kt.at[rel, part], kt.at[rel, part], dy=dy)
-                copy.start()
-                second.append(copy)
+                moves.append((kt.at[rel, part], kt.at[rel, part], dict(dy=dy)))
+    second = together(kt.at[pl.ds(1, 2), pl.ds(0, 3 * QUARTER)], moves)
+    ready = iter(second.copies)
+    for at in range(len(PIECES)):
+        for rel in (1, 2):
+            first[rel, at].wait_recv()
+            for _ in range(3):
+                next(ready).start()
 
     swap_q.wait_recv()
     swap_do.wait_recv()
@@ -157,8 +188,7 @@
 
     keys_in(0)
     score(0, 1)
-    for copy in second:
-        copy.wait_recv()
+    second.wait_recv()
     for rel in (1, 2):
         keys_in(rel)
     score(1, 2)
@@ -216,7 +246,14 @@
         for g in range(groups):
             rel = start + g
             full = dv[g * 128 : g * 128 + 128]
-            h1[rel] = full[:, :COLS_Y].astype(BF16)
+            first_tiles = full[:, :COLS_Y].astype(BF16)
+            if rel > 0:
+                h1[rel - 1] = first_tiles
+            else:
+                for t in range(3):
+                    near = dot(by_z, first_tiles[:, t * 128 : t * 128 + 128]).astype(BF16)
+                    for l in range(ZL):
+                        h3[l, t * 32 : t * 32 + 32, :] = near[l * 32 : l * 32 + 32, :]
             main = dot(by_z, full[:, COLS_Y:].astype(BF16)).astype(BF16)
             rope = dk[g * 128 : g * 128 + 128, LATENT:].astype(BF16)
             low = dot(by_z_low, rope)
@@ -225,11 +262,6 @@
             for l in range(ZL):
                 h2[rel, l, 0:32, :] = main[l * 32 : l * 32 + 32, :]
                 h2[rel, l, 32:48, :] = side[l * 16 : l * 16 + 16, :]
-            if rel == 0:
-                for t in (1, 2):
-                    near = dot(by_z, h1[0, :, t * 128 : t * 128 + 128]).astype(BF16)
-                    for l in range(ZL):
-                        h3[l, t * 32 - 32 : t * 32, :] = near[l * 32 : l * 32 + 32, :]
             keys = kr[rel, :, :LATENT].astype(F32)
             gain = gain + jnp.sum(full * keys, axis=0, keepdims=True)
         return gain
@@ -247,26 +279,26 @@
         return (z // ZL + ZH - zh) % ZH, z % ZL
 
     gain = key_part(1, 2, gain)
-    stage_z = [remote(h2.at[z_at(d)], h2_in.at[i], dz=d) for i, d in enumerate(Z_PEERS)]
-    stage_y = [
-        remote(h1.at[pl.ds(1, 2), y_rows(d), :], h1_in.at[i, pl.ds(1, 2)], dy=d)
-        for i, d in enumerate(Y_PEERS)
-    ]
-    for i, copy in enumerate(stage_y):
+    stage_z = together(
+        h2_in, [(h2.at[z_at(d)], h2_in.at[i], dict(dz=d)) for i, d in enumerate(Z_PEERS)]
+    )
+    stage_y = together(
+        h1_in, [(h1.at[:, y_rows(d), :], h1_in.at[i], dict(dy=d)) for i, d in enumerate(Y_PEERS)]
+    )
+    for i, copy in enumerate(stage_y.copies):
         copy.start()
         if i < Z_FAR:
-            stage_z[i].start()
+            stage_z.copies[i].start()
     gain = key_part(0, 1, gain)
-    stage_l = [remote(h3.at[(zl + d) % ZL], h3_in.at[d - 1], dl=d) for d in (1, 2, 3)]
-    last_y = [
-        remote(h1.at[0, y_rows(d), pl.ds(0, 128)], h1_in.at[i, 0, :, pl.ds(0, 128)], dy=d)
-        for i, d in enumerate(Y_PEERS)
-    ]
+    stage_l = together(
+        h3_in, [(h3.at[(zl + d) % ZL], h3_in.at[d - 1], dict(dl=d)) for d in (1, 2, 3)]
+    )
     pack(gain, ga)
-    gain_a = [remote(ga, ga_in.at[i], dx=d, dc=c) for i, (d, c) in enumerate(X_PEERS)]
-    for copy in stage_z[Z_FAR:] + stage_l + last_y + gain_a:
+    gain_a = together(
+        ga_in, [(ga, ga_in.at[i], dict(dx=d, dc=c)) for i, (d, c) in enumerate(X_PEERS)]
+    )
+    for copy in stage_z.copies[Z_FAR:] + stage_l.copies + gain_a.copies:
         copy.start()
-    stage_y = stage_y + last_y
 
     def query_part(cc):
         total = dot(kt[0], ds[cc, 0:128, :])
@@ -277,53 +309,50 @@
     swap_dq = []
     for cc in (2, 3):
         dq[cc - 2] = query_part(cc)
-        copy = remote(dq.at[cc - 2], dq_in.at[cc - 2], dc=1)
-        copy.start()
-        swap_dq.append(copy)
-
-    for copy in gain_a:
-        copy.wait_recv()
+        swap_dq.append(remote(dq.at[cc - 2], dq_in.at[cc - 2], dc=1))
+
+    gain_a.wait_recv()
     total = ga[...]
     for i in range(len(X_PEERS)):
         total = total + ga_in[i]
     gb[...] = total
-    gain_b = [remote(gb, gb_in.at[i], dy=d) for i, d in enumerate(Y_PEERS)]
-    for copy in gain_b:
+    gain_b = together(gb_in, [(gb, gb_in.at[i], dict(dy=d)) for i, d in enumerate(Y_PEERS)])
+    for copy in gain_b.copies + swap_dq:
         copy.start()
 
     for cc in range(2):
         dq_own[cc] = query_part(cc)
 
     t1[...] = jnp.zeros_like(t1)
-    for copy in stage_y:
-        copy.wait_recv()
-    for rel in range(3):
-        tiles = 3 if rel else 1
-        part = h1[rel, y_rows(0), : tiles * 128].astype(F32)
+    t2[...] = jnp.zeros_like(t2)
+    stage_y.wait_recv()
+    for rel in range(2):
+        part = h1[rel, y_rows(0), :].astype(F32)
         for i in range(len(Y_PEERS)):
-            part = part + h1_in[i, rel, :, : tiles * 128].astype(F32)
+            part = part + h1_in[i, rel].astype(F32)
         for l in range(ZL):
-            for t in range(tiles):
+            for t in range(3):
                 t1[rel, l, t * 4 : t * 4 + 4, :] = part[l * 4 : l * 4 + 4, t * 128 : (t + 1) * 128]
     h1b[...] = t1[...].astype(BF16)
-    stage_yz = [
-        remote(h1b.at[z_at(d)], h1b_in.at[i], dz=d) for i, d in enumerate(Z_PEERS)
-    ]
-    for copy in stage_yz:
-        copy.start()
-
-    for copy in gain_b:
-        copy.wait_recv()
+    stage_yz = together(
+        h1b_in,
+        [
+            (h1b.at[rel - 1, (zl + d) % ZL], h1b_in.at[i], dict(dz=rel * ZL, dl=d))
+            for i, (rel, d) in enumerate(OTHER_GROUPS)
+        ],
+    )
+    stage_yz.start()
+
+    gain_b.wait_recv()
     total = gb[...]
     for i in range(len(Y_PEERS)):
         total = total + gb_in[i]
     gc[...] = total
-    gain_c = [remote(gc, gc_in.at[i], dz=d) for i, d in enumerate(Z_PEERS)]
-    for copy in gain_c:
-        copy.start()
-
-    for copy in stage_z + stage_l:
-        copy.wait_recv()
+    gain_c = together(gc_in, [(gc, gc_in.at[i], dict(dz=d)) for i, d in enumerate(Z_PEERS)])
+    gain_c.start()
+
+    stage_z.wait_recv()
+    stage_l.wait_recv()
     part = h2[0, zl].astype(F32)
     for i in range(len(Z_PEERS)):
         part = part + h2_in[i].astype(F32)
@@ -333,12 +362,13 @@
     for yy in range(Y):
         t2[yy, 0:4, :] = part[yy * 4 : yy * 4 + 4, :]
         t2[yy, 4:8, :] = part[32 + (yy % 4) * 4 : 36 + (yy % 4) * 4, :]
-        t2[yy, 8:12, :] = near[yy * 4 : yy * 4 + 4, :]
-        t2[yy, 12:16, :] = near[32 + yy * 4 : 36 + yy * 4, :]
+        for t in range(3):
+            t2[yy, 8 + t * 4 : 12 + t * 4, :] = near[t * 32 + yy * 4 : t * 32 + yy * 4 + 4, :]
     t2b[...] = t2[...].astype(BF16)
-    stage_zy = [remote(t2b.at[(y + d) % Y], t2_in.at[i], dy=d) for i, d in enumerate(Y_PEERS)]
-    for copy in stage_zy:
-        copy.start()
+    stage_zy = together(
+        t2_in, [(t2b.at[(y + d) % Y], t2_in.at[i], dict(dy=d)) for i, d in enumerate(Y_PEERS)]
+    )
+    stage_zy.start()
 
     for cc in range(2):
         swap_dq[cc].wait_recv()
@@ -346,35 +376,31 @@
         gq_ref[cc * 2] = full[:, :128]
         gq_ref[cc * 2 + 1] = full[:, 128:]
 
-    for copy in stage_zy:
-        copy.wait_recv()
+    sent = list(first.values()) + [second, swap_q, swap_do, swap_stat] + swap_dq
+    sent += [stage_y, stage_z, stage_l, stage_yz, stage_zy, gain_a, gain_b, gain_c]
+    for copies in sent:
+        copies.wait_send()
+
+    stage_zy.wait_recv()
     late = t2[y]
     for i in range(len(Y_PEERS)):
         late = late + t2_in[i].astype(F32)
     gk_ref[:, COLS_Y:LATENT] = late[0:4, :]
     gk_ref[:, LATENT:] = jnp.where(y < Y // 2, late[4:8, :ROPE], late[4:8, ROPE:])
-    for copy in stage_yz:
-        copy.wait_recv()
-    part = t1[0, zl]
-    for i in range(len(Z_PEERS)):
-        part = part + h1b_in[i].astype(F32)
-    gk_ref[:, 0:128] = part[0:4, :]
-    gk_ref[:, 128:256] = part[4:8, :] + late[8:12, :]
-    gk_ref[:, 256:COLS_Y] = part[8:12, :] + late[12:16, :]
-    for copy in gain_c:
-        copy.wait_recv()
+    stage_yz.wait_recv()
+    part = late[8:20, :]
+    for i in range(len(OTHER_GROUPS)):
+        part = part + h1b_in[i, 0:12, :].astype(F32)
+    for t in range(3):
+        gk_ref[:, t * 128 : (t + 1) * 128] = part[t * 4 : t * 4 + 4, :]
+    gain_c.wait_recv()
     total = gc[...]
     for i in range(len(Z_PEERS)):
         total = total + gc_in[i]
     gg_ref[...] = total[0:4, :] / gain_ref[...]
 
-    sent = list(first.values()) + second + [swap_q, swap_do, swap_stat] + swap_dq
-    sent += gain_a + gain_b + gain_c + stage_y + stage_z + stage_l + stage_yz + stage_zy
-    for copy in sent:
-        copy.wait_send()
-
-
-N_COPIES = 4 + 12 + 3 + 2 + len(X_PEERS) + 4 * len(Y_PEERS) + 3 * len(Z_PEERS) + 3
+
+N_COPIES = 4 + 5 + 9
 
 
 def finish(gq_in, gk_in, gg_in, gq_out, gk_out, gg_out, sem):
@@ -417,18 +443,18 @@
             pltpu.VMEM((4, 384, 256), BF16),
             pltpu.VMEM((4, 8, 256), F32),
             pltpu.VMEM((4, 8, 256), F32),
-            pltpu.VMEM((3, 128, COLS_Y), BF16),
+            pltpu.VMEM((2, 128, COLS_Y), BF16),
             pltpu.VMEM((3, ZL, 48, 128), BF16),
-            pltpu.VMEM((ZL, 64, 128), BF16),
-            pltpu.VMEM((ny, 3, 16, COLS_Y), BF16),
+            pltpu.VMEM((ZL, 96, 128), BF16),
+            pltpu.VMEM((ny, 2, 16, COLS_Y), BF16),
             pltpu.VMEM((nz, 48, 128), BF16),
-            pltpu.VMEM((ZL - 1, 64, 128), BF16),
-            pltpu.VMEM((3, ZL, 16, 128), F32),
-            pltpu.VMEM((3, ZL, 16, 128), BF16),
-            pltpu.VMEM((nz, 16, 128), BF16),
-            pltpu.VMEM((Y, 16, 128), F32),
-            pltpu.VMEM((Y, 16, 128), BF16),
-            pltpu.VMEM((ny, 16, 128), BF16),
+            pltpu.VMEM((ZL - 1, 96, 128), BF16),
+            pltpu.VMEM((2, ZL, 16, 128), F32),
+            pltpu.VMEM((2, ZL, 16, 128), BF16),
+            pltpu.VMEM((len(OTHER_GROUPS), 16, 128), BF16),
+            pltpu.VMEM((Y, 32, 128), F32),
+            pltpu.VMEM((Y, 32, 128), BF16),
+            pltpu.VMEM((ny, 32, 128), BF16),
             pltpu.VMEM((8, 128), F32),
             pltpu.VMEM((nx, 8, 128), F32),
             pltpu.VMEM((8, 128), F32),

time: 50 us -> 48.4 us (0.968)
  Pallas kernels: 49.3 us -> 47.6 us
    pallas_call x1, Pallas kernels: 48.4 us -> 46.7 us  [body(): pl.pallas_call(kernel, out_shape=results, in_specs=[any_spec] * 5, out_sp...]
where the time goes in v6:
time: 48.4 us; the launch traced here: 48.2 us
  Pallas kernels  47.6 us (98%)
  between operations  0.64 us (1%)
    pallas_call x1, Pallas kernels, body(): pl.pallas_call(kernel, out_shape=results, in_specs=[any_spec] * 5, out_sp...  46.7 us

profile of v6, /device:TPU:1, one launch (start us, length us, event | category | flops | bytes accessed | tf_op | source)
XLA Modules:
  0.0 48.2 jit_solution(4979632868370504640)
XLA Ops:
  0.6 46.7 %mla_backward.1 = (bf16[4,576,128]{2,1,0:T(8,128)(2,1)S(1)}, f32[4,576]{1,0:T(4,128)S(1)}, f32[4,128]{1,0:T(4,128)S(1)}) custom-call(bf16[4,576,128]{2,1,0:T(8,128)(2,1)} %bitcast.13, bf16[128,4,512]{2,1,0:T(4,128)(2,1)} %bitcast.15, bf16[576,128]{1,0:T(8,128)(2,1)} %bitcast.16, f32[4,128]{1,0:T(4,128)} %bitcast.18, s32[1,6]{1,0:T(1,128)} %groups_hbm.1), custom_call_target="tpu_custom_call" | custom-call | flops 2162688000 | bytes 3145728 | tf_op jit(solution)/shard_map/mla_backward/pallas_call | solution.py:428
  47.4 0.9 %results.1 = (bf16[4,576,128]{2,1,0:T(8,128)(2,1)}, f32[4,576]{1,0:T(4,128)}, f32[4,128]{1,0:T(4,128)}) custom-call(bf16[4,576,128]{2,1,0:T(8,128)(2,1)S(1)} %get-tuple-element.9.gq_in, f32[4,576]{1,0:T(4,128)S(1)} %get-tuple-element.10.gk_in, f32[4,128]{1,0:T(4,128)S(1)} %get-tuple-element.11.gg_in), custom_call_target="tpu_custom_call" | custom-call | tf_op jit(solution)/shard_map/results/pallas_call | solution.py:481

commit v7 on v6

--- a/solution.py
+++ b/solution.py
@@ -21,7 +21,6 @@
 PIECES = ((0, 80), (80, 64))
 Y_PEERS = (4, 3, 5, 2, 6, 1, 7)
 Z_PEERS = (6, 5, 7, 4, 8, 3, 9, 2, 10, 1, 11)
-Z_FAR = 5
 OTHER_GROUPS = tuple((rel, d) for rel in (1, 2) for d in range(ZL))
 X_PEERS = ((0, 1), (1, 0), (3, 0), (2, 0), (1, 1), (3, 1), (2, 1))
 COLS_Y = 384
@@ -246,22 +245,23 @@
         for g in range(groups):
             rel = start + g
             full = dv[g * 128 : g * 128 + 128]
-            first_tiles = full[:, :COLS_Y].astype(BF16)
-            if rel > 0:
-                h1[rel - 1] = first_tiles
-            else:
-                for t in range(3):
-                    near = dot(by_z, first_tiles[:, t * 128 : t * 128 + 128]).astype(BF16)
-                    for l in range(ZL):
-                        h3[l, t * 32 : t * 32 + 32, :] = near[l * 32 : l * 32 + 32, :]
+            low_tiles = full[:, :COLS_Y].astype(BF16)
             main = dot(by_z, full[:, COLS_Y:].astype(BF16)).astype(BF16)
             rope = dk[g * 128 : g * 128 + 128, LATENT:].astype(BF16)
             low = dot(by_z_low, rope)
             high = dot(by_z_high, rope)
             side = jnp.concatenate([low, high], axis=1).astype(BF16)
+            if rel > 0:
+                h1[rel - 1] = low_tiles
             for l in range(ZL):
-                h2[rel, l, 0:32, :] = main[l * 32 : l * 32 + 32, :]
-                h2[rel, l, 32:48, :] = side[l * 16 : l * 16 + 16, :]
+                to = h2.at[rel - 1, l] if rel > 0 else h3.at[l]
+                to[0:32, :] = main[l * 32 : l * 32 + 32, :]
+                to[32:48, :] = side[l * 16 : l * 16 + 16, :]
+            if rel == 0:
+                for t in range(3):
+                    near = dot(by_z, low_tiles[:, t * 128 : t * 128 + 128]).astype(BF16)
+                    for l in range(ZL):
+                        h3[l, 48 + t * 32 : 80 + t * 32, :] = near[l * 32 : l * 32 + 32, :]
             keys = kr[rel, :, :LATENT].astype(F32)
             gain = gain + jnp.sum(full * keys, axis=0, keepdims=True)
         return gain
@@ -274,22 +274,17 @@
     def y_rows(dy):
         return pl.ds(pl.multiple_of(((y + dy) % Y) * 16, 16), 16)
 
-    def z_at(dz):
-        z = (zh * ZL + zl + dz) % (ZH * ZL)
-        return (z // ZL + ZH - zh) % ZH, z % ZL
-
-    gain = key_part(1, 2, gain)
+    gain = key_part(0, 3, gain)
     stage_z = together(
-        h2_in, [(h2.at[z_at(d)], h2_in.at[i], dict(dz=d)) for i, d in enumerate(Z_PEERS)]
+        h2_in,
+        [
+            (h2.at[rel - 1, (zl + d) % ZL], h2_in.at[i], dict(dz=rel * ZL, dl=d))
+            for i, (rel, d) in enumerate(OTHER_GROUPS)
+        ],
     )
     stage_y = together(
         h1_in, [(h1.at[:, y_rows(d), :], h1_in.at[i], dict(dy=d)) for i, d in enumerate(Y_PEERS)]
     )
-    for i, copy in enumerate(stage_y.copies):
-        copy.start()
-        if i < Z_FAR:
-            stage_z.copies[i].start()
-    gain = key_part(0, 1, gain)
     stage_l = together(
         h3_in, [(h3.at[(zl + d) % ZL], h3_in.at[d - 1], dict(dl=d)) for d in (1, 2, 3)]
     )
@@ -297,8 +292,12 @@
     gain_a = together(
         ga_in, [(ga, ga_in.at[i], dict(dx=d, dc=c)) for i, (d, c) in enumerate(X_PEERS)]
     )
-    for copy in stage_z.copies[Z_FAR:] + stage_l.copies + gain_a.copies:
-        copy.start()
+    for pair in zip(stage_z.copies, stage_y.copies):
+        for copy in pair:
+            copy.start()
+    stage_z.copies[-1].start()
+    gain_a.start()
+    stage_l.start()
 
     def query_part(cc):
         total = dot(kt[0], ds[cc, 0:128, :])
@@ -353,17 +352,17 @@
 
     stage_z.wait_recv()
     stage_l.wait_recv()
-    part = h2[0, zl].astype(F32)
-    for i in range(len(Z_PEERS)):
-        part = part + h2_in[i].astype(F32)
     near = h3[zl].astype(F32)
     for i in range(ZL - 1):
         near = near + h3_in[i].astype(F32)
+    part = near[0:48, :]
+    for i in range(len(OTHER_GROUPS)):
+        part = part + h2_in[i].astype(F32)
     for yy in range(Y):
         t2[yy, 0:4, :] = part[yy * 4 : yy * 4 + 4, :]
         t2[yy, 4:8, :] = part[32 + (yy % 4) * 4 : 36 + (yy % 4) * 4, :]
         for t in range(3):
-            t2[yy, 8 + t * 4 : 12 + t * 4, :] = near[t * 32 + yy * 4 : t * 32 + yy * 4 + 4, :]
+            t2[yy, 8 + t * 4 : 12 + t * 4, :] = near[48 + t * 32 + yy * 4 : 52 + t * 32 + yy * 4, :]
     t2b[...] = t2[...].astype(BF16)
     stage_zy = together(
         t2_in, [(t2b.at[(y + d) % Y], t2_in.at[i], dict(dy=d)) for i, d in enumerate(Y_PEERS)]
@@ -444,11 +443,11 @@
             pltpu.VMEM((4, 8, 256), F32),
             pltpu.VMEM((4, 8, 256), F32),
             pltpu.VMEM((2, 128, COLS_Y), BF16),
-            pltpu.VMEM((3, ZL, 48, 128), BF16),
-            pltpu.VMEM((ZL, 96, 128), BF16),
+            pltpu.VMEM((2, ZL, 48, 128), BF16),
+            pltpu.VMEM((ZL, 144, 128), BF16),
             pltpu.VMEM((ny, 2, 16, COLS_Y), BF16),
-            pltpu.VMEM((nz, 48, 128), BF16),
-            pltpu.VMEM((ZL - 1, 96, 128), BF16),
+            pltpu.VMEM((len(OTHER_GROUPS), 48, 128), BF16),
+            pltpu.VMEM((ZL - 1, 144, 128), BF16),
             pltpu.VMEM((2, ZL, 16, 128), F32),
             pltpu.VMEM((2, ZL, 16, 128), BF16),
             pltpu.VMEM((len(OTHER_GROUPS), 16, 128), BF16),

time: 48.4 us -> 48 us (level)
  no operation moved by 1% of the time
where the time goes in v7:
time: 48 us; the launch traced here: 47.9 us
  Pallas kernels  47.2 us (98%)
  between operations  0.64 us (1%)
    pallas_call x1, Pallas kernels, body(): pl.pallas_call(kernel, out_shape=results, in_specs=[any_spec] * 5, out_sp...  46.4 us

profile of v7, /device:TPU:1, one launch (start us, length us, event | category | flops | bytes accessed | tf_op | source)
XLA Modules:
  0.0 47.9 jit_solution(15388645808017462525)
XLA Ops:
  0.6 46.4 %mla_backward.1 = (bf16[4,576,128]{2,1,0:T(8,128)(2,1)S(1)}, f32[4,576]{1,0:T(4,128)S(1)}, f32[4,128]{1,0:T(4,128)S(1)}) custom-call(bf16[4,576,128]{2,1,0:T(8,128)(2,1)} %bitcast.13, bf16[128,4,512]{2,1,0:T(4,128)(2,1)} %bitcast.15, bf16[576,128]{1,0:T(8,128)(2,1)} %bitcast.16, f32[4,128]{1,0:T(4,128)} %bitcast.18, s32[1,6]{1,0:T(1,128)} %groups_hbm.1), custom_call_target="tpu_custom_call" | custom-call | flops 2162688000 | bytes 3145728 | tf_op jit(solution)/shard_map/mla_backward/pallas_call | solution.py:427
  47.0 0.9 %results.1 = (bf16[4,576,128]{2,1,0:T(8,128)(2,1)}, f32[4,576]{1,0:T(4,128)}, f32[4,128]{1,0:T(4,128)}) custom-call(bf16[4,576,128]{2,1,0:T(8,128)(2,1)S(1)} %get-tuple-element.9.gq_in, f32[4,576]{1,0:T(4,128)S(1)} %get-tuple-element.10.gk_in, f32[4,128]{1,0:T(4,128)S(1)} %get-tuple-element.11.gg_in), custom_call_target="tpu_custom_call" | custom-call | tf_op jit(solution)/shard_map/results/pallas_call | solution.py:480

commit v8 on v7

--- a/solution.py
+++ b/solution.py
@@ -178,8 +178,8 @@
                 visible = diff <= (group[cc // 2] - base) * 128
                 s = jnp.where(visible, raw[g * 128 : g * 128 + 128], MASKED)
                 dp = grad[g * 128 : g * 128 + 128]
-                m = jnp.max(s, axis=0, keepdims=True)
-                p = jnp.where(visible, jnp.exp(s - m), 0.0)
+                m = jnp.maximum(jnp.max(s, axis=0, keepdims=True), 0.1 * MASKED)
+                p = jnp.exp(s - m)
                 st[cc, rel * 128 : rel * 128 + 128, :] = p
                 parts[rel, cc] = (
                     m, jnp.sum(p, axis=0, keepdims=True), jnp.sum(p * dp, axis=0, keepdims=True)

time: 48 us -> 48 us (level)
  no operation moved by 1% of the time
where the time goes in v8:
time: 48 us; the launch traced here: 47.8 us
  Pallas kernels  47.2 us (98%)
  between operations  0.64 us (1%)
    pallas_call x1, Pallas kernels, body(): pl.pallas_call(kernel, out_shape=results, in_specs=[any_spec] * 5, out_sp...  46.3 us

profile of v8, /device:TPU:1, one launch (start us, length us, event | category | flops | bytes accessed | tf_op | source)
XLA Modules:
  0.0 47.8 jit_solution(9499346313617770764)
XLA Ops:
  0.6 46.3 %mla_backward.1 = (bf16[4,576,128]{2,1,0:T(8,128)(2,1)S(1)}, f32[4,576]{1,0:T(4,128)S(1)}, f32[4,128]{1,0:T(4,128)S(1)}) custom-call(bf16[4,576,128]{2,1,0:T(8,128)(2,1)} %bitcast.13, bf16[128,4,512]{2,1,0:T(4,128)(2,1)} %bitcast.15, bf16[576,128]{1,0:T(8,128)(2,1)} %bitcast.16, f32[4,128]{1,0:T(4,128)} %bitcast.18, s32[1,6]{1,0:T(1,128)} %groups_hbm.1), custom_call_target="tpu_custom_call" | custom-call | flops 2162688000 | bytes 3145728 | tf_op jit(solution)/shard_map/mla_backward/pallas_call | solution.py:427
  46.9 0.9 %results.1 = (bf16[4,576,128]{2,1,0:T(8,128)(2,1)}, f32[4,576]{1,0:T(4,128)}, f32[4,128]{1,0:T(4,128)}) custom-call(bf16[4,576,128]{2,1,0:T(8,128)(2,1)S(1)} %get-tuple-element.9.gq_in, f32[4,576]{1,0:T(4,128)S(1)} %get-tuple-element.10.gk_in, f32[4,128]{1,0:T(4,128)S(1)} %get-tuple-element.11.gg_in), custom_call_target="tpu_custom_call" | custom-call | tf_op jit(solution)/shard_map/results/pallas_call | solution.py:480
